TPU v7x, 32 devices: a whole 2x2x4 slice. The times are simulated.
32 devices in a mesh: dp: 16 (over z, y, core), slab: 2 (over x).
Axes of the slice: x: 2, y: 2, z: 4, core: 2. Of those that a mesh axis runs over, the one named last changes fastest.
Arguments:
- snapshots: bfloat16 [16, 64, 512, 512], P('dp', None, 'slab'), may hold values from -6 to 6
- cotangent: bfloat16 [16, 64, 512, 512], P('dp', None, 'slab'), may hold values from -6 to 6
- w_spec: float32 [32, 32, 64, 128], P('slab', 'dp'), may hold values from -0.5 to 0.5
- first_moment: float32 [32, 32, 64, 128], P('slab', 'dp'), may hold values from -6 to 6
- second_moment: float32 [32, 32, 64, 128], P('slab', 'dp'), may hold values from 0.1 to 4
- w_skip: bfloat16 [64, 64], replicated, may hold values from -0.75 to 0.75
- bias: float32 [64], replicated, may hold values from -3 to 3
Outputs:
- layer_out: bfloat16 [16, 64, 512, 512], P('dp', None, 'slab')
- new_weights: float32 [32, 32, 64, 128], P('slab', 'dp')
- new_first: float32 [32, 32, 64, 128], P('slab', 'dp')
- new_second: float32 [32, 32, 64, 128], P('slab', 'dp')
All inputs are finite; a program needn't handle non-finite values.
Results may differ from a plain program's by a relative error of at most 0.001.
Values sent between devices are 32-bit elements; how exact they have to be, the bound alone decides.
A program may use at most 192 MiB of HBM per device.

v0:
```python
import functools
import math

import jax
import jax.numpy as jnp
import ml_dtypes
import numpy as np
from jax import lax
from jax.experimental import pallas as pl
from jax.experimental.pallas import tpu as pltpu
from jax.sharding import PartitionSpec as P

NY = 512
NZ = 512
KY = 32
KZ = 32
ROWS = 16
SUB = 8

high = lax.Precision.HIGHEST
gelu_coef = 0.7978845608028654
cube_coef = 0.044715
vmem_bytes = 56 * 1024 * 1024


def halves(table):
    top = table.astype(ml_dtypes.bfloat16)
    rest = (table - top.astype(np.float64)).astype(ml_dtypes.bfloat16)
    return top, rest


def z_table():
    angle = 2.0 * math.pi / NZ * (np.outer(np.arange(NZ), np.arange(KZ)) % NZ)
    return np.concatenate([np.cos(angle), -np.sin(angle)], 1)


def y_table():
    freq = np.concatenate([np.arange(KY // 2), np.arange(KY // 2) - KY // 2])
    angle = 2.0 * math.pi / NY * (np.outer(np.arange(NY), freq) % NY)
    return np.concatenate([np.cos(angle), np.sin(angle)], 1)


def split(x):
    top = x.astype(jnp.bfloat16)
    return top, (x - top.astype(jnp.float32)).astype(jnp.bfloat16)


def mm(a, b):
    return jnp.dot(a, b, preferred_element_type=jnp.float32)


def one_hot(shape, test):
    rows = lax.broadcasted_iota(jnp.int32, shape, 0)
    columns = lax.broadcasted_iota(jnp.int32, shape, 1)
    return jnp.where(test(rows, columns), 1.0, 0.0).astype(jnp.bfloat16)


def each(count, step):
    per = 8

    @pl.loop(0, count // per)
    def _(i):
        for n in range(per):
            step(i * per + n)


def y_modes(zval, ytab):
    top, rest = split(zval)
    both = mm(ytab, jnp.concatenate([top, rest], axis=1))
    first = both[: 2 * KY]
    w = first[:, : 2 * KZ] + first[:, 2 * KZ :] + both[2 * KY :, : 2 * KZ]
    real = w[:KY, :KZ] + w[KY:, KZ:]
    imag = w[:KY, KZ:] - w[KY:, :KZ]
    return jnp.concatenate([real, imag], axis=1)


def forward_kernel(x_ref, zt_ref, yt_ref, o_ref):
    per, rows, length = x_ref.shape
    zval = mm(x_ref[...].reshape(per * rows, length), zt_ref[...])
    zval = (zval[:, : 2 * KZ] + zval[:, 2 * KZ :]).reshape(per, rows, 2 * KZ)
    for c in range(per):
        o_ref[c] = y_modes(zval[c], yt_ref[...])


def point_kernel(
    x_ref, cot_ref, spec_ref, bias_ref, skip_ref, zt_ref, yt_ref, back_ref, yback_ref,
    out_ref, g_ref, left, zsum, kron_ref,
):
    step = pl.program_id(0)
    chans, rows = left.shape[:2]
    wide = 2 * KZ

    @pl.when(step == 0)
    def _():
        tall = chans * SUB
        part = tall // 4
        spread = one_hot((chans, tall), lambda i, r: i == r // SUB)
        for m in range(4):
            pick = one_hot((part, chans), lambda r, o: (r + m * part) // SUB == o)
            rows_of = mm(pick, skip_ref[...]).astype(jnp.bfloat16)
            same = one_hot((part, tall), lambda r, s: r % SUB == s % SUB)
            kron_ref[m * part : (m + 1) * part, :] = (
                mm(rows_of, spread).astype(jnp.bfloat16) * same
            )

        def invert(o):
            v = spec_ref[o]
            turned = jnp.concatenate([-v[:, KZ:], v[:, :KZ]], axis=1)
            top, rest = split(jnp.concatenate([v, turned], axis=0))
            yval = mm(yback_ref[...], jnp.concatenate([top, rest, top], axis=0))
            ytop, yrest = split(yval)
            b = bias_ref[o]
            b0 = b.astype(jnp.bfloat16).astype(jnp.float32)
            b1 = (b - b0).astype(jnp.bfloat16).astype(jnp.float32)
            lane = lax.broadcasted_iota(jnp.int32, b.shape, 1)
            terms = jnp.where(lane == 0, b0, jnp.where(lane == 1, b1, b - b0 - b1))
            terms = jnp.broadcast_to(terms, (rows, wide)).astype(jnp.bfloat16)
            left[o] = jnp.concatenate([ytop, yrest, ytop, terms], axis=1)

        each(chans, invert)

    here = pl.ds(pl.multiple_of(step * ROWS, ROWS), ROWS)
    field = x_ref[...].astype(jnp.float32)
    terms = left[:, here, :].astype(jnp.float32)
    values = []
    for m in range(ROWS // SUB):
        own = slice(m * SUB, (m + 1) * SUB)
        x = field[:, own].reshape(chans * SUB, NZ).astype(jnp.bfloat16)
        term = terms[:, own].reshape(chans * SUB, 4 * wide).astype(jnp.bfloat16)
        pre = mm(kron_ref[...], x) + mm(term, back_ref[...])
        sq = pre * pre
        t = jnp.tanh(pre * (gelu_coef + (gelu_coef * cube_coef) * sq))
        h = 0.5 + 0.5 * t
        value = pre * h
        values.append(value.reshape(chans, SUB, NZ))
        grow = 2.0 * gelu_coef + (6.0 * gelu_coef * cube_coef) * sq
        cot = cot_ref[...].astype(jnp.float32)[:, own].reshape(chans * SUB, NZ)
        slope = cot * (h + value * (0.5 - 0.5 * t) * grow)
        top, rest = split(slope)
        zval = mm(top, zt_ref[...])
        zval = zval[:, :wide] + zval[:, wide:] + mm(rest, zt_ref[:, :wide])
        place = pl.ds(pl.multiple_of(step * ROWS + m * SUB, SUB), SUB)
        zsum[:, place, :] = zval.reshape(chans, SUB, wide)
    out_ref[...] = jnp.concatenate(values, axis=1).astype(jnp.bfloat16)

    @pl.when(step == pl.num_programs(0) - 1)
    def _():
        def forward(o):
            g_ref[o] = y_modes(zsum[o], yt_ref[...])

        each(chans, forward)


def whole(shape):
    return pl.BlockSpec(shape, lambda i: (0,) * len(shape))


def forward_modes(field, zt, yt):
    chans, rows, length = field.shape
    per = 8
    return pl.pallas_call(
        forward_kernel,
        grid=(chans // per,),
        in_specs=[
            pl.BlockSpec((per, rows, length), lambda i: (i, 0, 0)),
            whole(zt.shape),
            whole(yt.shape),
        ],
        out_specs=pl.BlockSpec((per, KY, 2 * KZ), lambda i: (i, 0, 0)),
        out_shape=jax.ShapeDtypeStruct((chans, KY, 2 * KZ), jnp.float32),
        compiler_params=pltpu.CompilerParams(vmem_limit_bytes=vmem_bytes),
    )(field, zt, yt)


def point_part(field, cot, spec, bias, skip, zt, yt, back, yback):
    chans, rows, length = field.shape
    rowed = pl.BlockSpec((chans, ROWS, length), lambda i: (0, i, 0))
    return pl.pallas_call(
        point_kernel,
        grid=(rows // ROWS,),
        in_specs=[rowed, rowed]
        + [whole(a.shape) for a in (spec, bias, skip, zt, yt, back, yback)],
        out_specs=[rowed, whole((chans, KY, 2 * KZ))],
        out_shape=[
            jax.ShapeDtypeStruct(field.shape, jnp.bfloat16),
            jax.ShapeDtypeStruct((chans, KY, 2 * KZ), jnp.float32),
        ],
        scratch_shapes=[
            pltpu.VMEM((chans, rows, 8 * KZ), jnp.bfloat16),
            pltpu.VMEM((chans, rows, 2 * KZ), jnp.float32),
            pltpu.VMEM((chans * SUB, chans * SUB), jnp.bfloat16),
        ],
        compiler_params=pltpu.CompilerParams(vmem_limit_bytes=vmem_bytes),
    )(field, cot, spec, bias, skip, zt, yt, back, yback)


def to_owner(modes, dp, slab):
    chans = modes.shape[0]
    x = modes.reshape(chans, dp, KY // dp, 2, slab, KZ // slab)
    x = x.transpose(1, 4, 5, 2, 3, 0).reshape(dp * slab, -1, chans)
    x = lax.all_to_all(x, ("dp", "slab"), split_axis=0, concat_axis=0, tiled=True)
    x = x.reshape(dp, slab, KZ // slab, KY // dp, 2, chans).sum(1)
    return x.transpose(1, 2, 0, 3, 4)


def from_owner(spec, dp, slab):
    chans = spec.shape[-1]
    x = spec.transpose(2, 0, 1, 3, 4).reshape(dp, 1, -1, chans)
    x = jnp.broadcast_to(x, (dp, slab) + x.shape[2:]).reshape(dp * slab, -1, chans)
    x = lax.all_to_all(x, ("dp", "slab"), split_axis=0, concat_axis=0, tiled=True)
    x = x.reshape(dp, slab, KZ // slab, KY // dp, 2, chans)
    return x.transpose(5, 0, 3, 4, 1, 2).reshape(chans, KY, 2 * KZ)


def body(snapshots, cotangent, w_spec, first_moment, second_moment, w_skip, bias):
    chans, rows, length = snapshots.shape[1:]
    spec_scale = 1.0 / math.sqrt(NY * NZ)
    out_scale = 1.0 / math.sqrt(KY * KZ)
    dp = lax.axis_size("dp")
    slab = lax.axis_size("slab")
    start = lax.axis_index("slab") * rows
    ztop, zrest = halves(z_table())
    ytop, yrest = halves(y_table())
    zt = jnp.asarray(np.concatenate([ztop, zrest], 1))
    ones = np.zeros((2 * KZ, length), ml_dtypes.bfloat16)
    ones[:3] = 1
    back = jnp.asarray(np.concatenate([ztop.T, ztop.T, zrest.T, ones], 0))
    yt = jnp.asarray(np.concatenate([ytop, yrest], 1).T)
    yt = lax.dynamic_slice_in_dim(yt, start, rows, 1)
    yback = jnp.asarray(np.concatenate([ytop, ytop, yrest], 1))
    yback = lax.dynamic_slice_in_dim(yback, start, rows, 0)
    bias_lanes = jnp.pad(
        jnp.broadcast_to(bias[:, None, None], (chans, 1, 3)), ((0, 0), (0, 0), (0, 2 * KZ - 3))
    )

    u = to_owner(forward_modes(snapshots[0], zt, yt), dp, slab) * spec_scale
    prod = jnp.einsum("kjbri,kjio->kjbro", u, w_spec, precision=high)
    vreal = prod[..., 0, :chans] - prod[..., 1, chans:]
    vimag = prod[..., 0, chans:] + prod[..., 1, :chans]
    spec = from_owner(jnp.stack([vreal, vimag], 3) * out_scale, dp, slab)
    layer_out, gmodes = point_part(
        snapshots[0], cotangent[0], spec, bias_lanes, w_skip.T, zt, yt, back, yback
    )
    g = to_owner(gmodes, dp, slab) * (out_scale / dp)
    turned = jnp.stack([g[..., 1, :], -g[..., 0, :]], 3)
    pair = jnp.concatenate([g, turned], -1)
    grad = jnp.einsum("kjbri,kjbro->kjio", u, pair, precision=high)
    new_first = 0.9 * first_moment + 0.1 * grad
    new_second = 0.95 * second_moment + 0.05 * grad * grad
    bias_first = 1.0 - 0.9**10
    bias_second = 1.0 - 0.95**10
    new_weights = w_spec - 0.01 * (new_first / bias_first) / (
        jnp.sqrt(new_second / bias_second) + 1e-08
    )
    return (layer_out[None], new_weights, new_first, new_second)


def solution(mesh):
    placed = (
        P("dp", None, "slab", None),
        P("dp", None, "slab", None),
        P("slab", "dp", None, None),
        P("slab", "dp", None, None),
        P("slab", "dp", None, None),
        P(),
        P(),
    )
    return jax.shard_map(
        body,
        mesh=mesh,
        in_specs=placed,
        out_specs=(
            P("dp", None, "slab", None),
            P("slab", "dp", None, None),
            P("slab", "dp", None, None),
            P("slab", "dp", None, None),
        ),
        check_vma=False,
    )
```

profile of v0, /device:TPU:1, one launch (start us, length us, event | category | flops | bytes accessed | tf_op | source)
XLA Modules:
  0.0 162.3 jit_solution(5828625482882387108)
XLA Ops:
  0.6 1.6 constant_dynamic-slice_fusion.1.yt_ref
  2.2 14.9 %shard_map.138 = f32[64,32,64]{2,1,0:T(8,128)} custom-call(bf16[64,256,512]{2,1,0:T(8,128)(2,1)} %bitcast.39, bf16[512,128]{1,0:T(8,128)(2,1)} %constant.43.clone.zt_ref, bf16[128,256]{1,0:T(8,128)(2,1)} %constant_dynamic-slice_fusion.1.yt_ref), custom_call_target="tpu_custom_call" | custom-call | tf_op jit(solution)/shard_map/pallas_call | solution.py:161
  17.1 1.8 %copy.25 = f32[64,32,64]{0,2,1:T(8,128)S(1)} copy(f32[64,32,64]{2,1,0:T(8,128)} %shard_map.138) | data formatting | bytes 1048576 | tf_op jit(solution)/shard_map/pallas_call | solution.py:161
  18.8 0.8 copy.26
  19.7 0.7 reshape.51
  20.3 22.7 %all_to_all.15 = f32[32,1,4096]{2,1,0:T(1,128)S(1)} all-to-all(f32[32,1,4096]{2,1,0:T(1,128)S(1)} %reshape.51), channel_id=1, replica_groups=mesh['dp'=16,'slab'=2] {'dp','slab'}, dimensions={0} | all-to-all | bytes 1048576 | tf_op jit(solution)/shard_map/all_to_all | solution.py:201
  43.0 0.6 broadcast.25
  43.6 1.9 %reduce = f32[32,4096]{1,0:T(8,128)S(1)} reduce(f32[32,1,4096]{2,1,0:T(1,128)S(1)} %all_to_all.15, f32[]{:T(128)} %broadcast.25), dimensions={1}, to_apply=%all_to_all.9.reduce_sub_computation | reduce | bytes 1048580 | tf_op jit(solution)/shard_map/all_to_all | solution.py:201
  45.6 0.4 reshape.52
  46.0 1.0 reduce_sum.18
  47.0 1.3 fusion.1
  48.4 0.2 slice_subtract_fusion
  49.0 1.4 reshape.53
  50.4 2.8 %all-to-all-start.1 = ((f32[32,1,4096]{2,1,0:T(1,128)}), f32[32,1,4096]{2,1,0:T(1,128)S(1)}, u32[]{:S(2)}, u32[]{:S(2)}) async-start(f32[32,1,4096]{2,1,0:T(1,128)} %reshape.53), calls=%async_computation.1 | async-start | bytes 1048576 | tf_op jit(solution)/shard_map/all_to_all | solution.py:210
  53.2 0.7 copy.30
  54.1 0.6 pad.4.bias_ref
  54.7 0.7 constant_dynamic-slice_fusion.yback_ref
  55.4 13.7 %all-to-all-done.1 = f32[32,1,4096]{2,1,0:T(1,128)S(1)} async-done(((f32[32,1,4096]{2,1,0:T(1,128)}), f32[32,1,4096]{2,1,0:T(1,128)S(1)}, u32[]{:S(2)}, u32[]{:S(2)}) %all-to-all-start.1) | async-done | bytes 524320 | tf_op jit(solution)/shard_map/all_to_all | solution.py:210
  69.0 1.9 %reduce.1 = f32[32,4096]{1,0:T(8,128)S(1)} reduce(f32[32,1,4096]{2,1,0:T(1,128)S(1)} %all-to-all-done.1, f32[]{:T(128)} %broadcast.25), dimensions={1}, to_apply=%all_to_all.10.reduce_sub_computation | reduce | bytes 1048580 | tf_op jit(solution)/shard_map/all_to_all | solution.py:210
  71.0 0.4 reshape.54
  71.4 1.1 copy.29
  72.5 3.0 %copy.31.spec_ref = f32[64,32,64]{2,1,0:T(8,128)} copy(f32[64,32,64]{0,2,1:T(8,128)} %bitcast.48) | data formatting | bytes 1048576 | tf_op jit(solution)/shard_map/reshape | solution.py:212
  75.5 53.3 %shard_map.139 = (bf16[64,256,512]{2,1,0:T(8,128)(2,1)}, f32[64,32,64]{2,1,0:T(8,128)}) custom-call(bf16[64,256,512]{2,1,0:T(8,128)(2,1)} %bitcast.40, bf16[64,256,512]{2,1,0:T(8,128)(2,1)} %bitcast.41, f32[64,32,64]{2,1,0:T(8,128)} %copy.31.spec_ref, f32[64,1,64]{2,1,0:T(1,128)} %pad.4.bias_ref, bf16[64,64]{1,0:T(8,128)(2,1)} %bitcast.52, ...), custom_call_target="tpu_custom_call" | custom-call | tf_op jit(solution)/shard_map/pallas_call | solution.py:178
  128.8 1.8 %copy.32 = f32[64,32,64]{0,2,1:T(8,128)S(1)} copy(f32[64,32,64]{2,1,0:T(8,128)} %get-tuple-element.7) | data formatting | bytes 1048576 | tf_op jit(solution)/shard_map/pallas_call | solution.py:178
  130.5 1.8 %copy.33 = f32[16,2,16,2,2,64]{5,4,3,2,1,0:T(2,128)} copy(f32[16,2,16,2,2,64]{5,2,1,4,3,0:T(8,128)S(1)} %bitcast.49) | data formatting | bytes 1048576 | tf_op jit(solution)/shard_map/transpose | solution.py:200
  132.3 1.9 %reshape.55 = f32[32,1,4096]{2,1,0:T(1,128)S(1)} reshape(f32[32,64,64]{2,1,0:T(8,128)} %bitcast.50) | data formatting | bytes 1048576
  134.2 18.4 %all_to_all.16 = f32[32,1,4096]{2,1,0:T(1,128)S(1)} all-to-all(f32[32,1,4096]{2,1,0:T(1,128)S(1)} %reshape.55), channel_id=1, replica_groups=mesh['dp'=16,'slab'=2] {'dp','slab'}, dimensions={0} | all-to-all | bytes 1048576 | tf_op jit(solution)/shard_map/all_to_all | solution.py:201
  152.6 1.9 %reduce.2 = f32[32,4096]{1,0:T(8,128)S(1)} reduce(f32[32,1,4096]{2,1,0:T(1,128)S(1)} %all_to_all.16, f32[]{:T(128)} %broadcast.25), dimensions={1}, to_apply=%all_to_all.11.reduce_sub_computation | reduce | bytes 1048580 | tf_op jit(solution)/shard_map/all_to_all | solution.py:201
  154.6 0.4 reshape.56
  155.0 1.0 reduce_sum.19
  156.0 0.3 fusion.10
  156.4 5.8 %divide_subtract_fusion = (f32[16,2,64,128]{3,2,1,0:T(8,128)}, f32[16,2,64,128]{3,2,1,0:T(8,128)}, f32[16,2,64,128]{3,2,1,0:T(8,128)}) fusion(f32[16,2,64,128]{3,2,1,0:T(8,128)S(1)} %copy-done, f32[16,2,64,128]{3,2,1,0:T(8,128)} %param.14, f32[16,2,64,128]{3,2,1,0:T(8,128)} %param.15, f32[16,2,16,1,64]{4,2,3,1,0:T(8,128)S(1)} %get-tuple-element.12, ...), kind=kOutput, calls=%fused_computation.5 | convolution fusion | flops 104136704 | bytes 7077888 | tf_op jit(solution)/shard_map/kjbri,kjbro->kjio/dot_general | solution.py:247
  (13 shorter events, 0.5 us)
Async XLA Ops:
  0.6 46.4 %copy-start = (f32[16,2,64,128]{3,2,1,0:T(8,128)S(1)}, f32[16,2,64,128]{3,2,1,0:T(8,128)}, u32[]{:S(2)}) copy-start(f32[16,2,64,128]{3,2,1,0:T(8,128)} %param.13) | copy-start | bytes 3145732
  2.2 51.0 %copy-start.2 = (bf16[64,64]{1,0:T(8,128)(2,1)S(1)}, bf16[64,64]{1,0:T(8,128)(2,1)}, u32[]{:S(2)}) copy-start(bf16[64,64]{1,0:T(8,128)(2,1)} %param.16) | copy-start | bytes 24580
  2.2 51.7 %copy-start.3 = (f32[64]{0:T(128)S(1)}, f32[64]{0:T(128)}, u32[]{:S(2)}) copy-start(f32[64]{0:T(128)} %param.17) | copy-start | bytes 772
  2.2 52.5 %copy-start.1 = (bf16[512,192]{1,0:T(8,128)(2,1)S(1)}, bf16[512,192]{1,0:T(8,128)(2,1)}, u32[]{:S(2)}) copy-start(bf16[512,192]{1,0:T(8,128)(2,1)} %constant.46.clone) | copy-start | bytes 589828
  50.4 18.6 %all-to-all-start.1 = ((f32[32,1,4096]{2,1,0:T(1,128)}), f32[32,1,4096]{2,1,0:T(1,128)S(1)}, u32[]{:S(2)}, u32[]{:S(2)}) async-start(f32[32,1,4096]{2,1,0:T(1,128)} %reshape.53), calls=%async_computation.1 | async-start | bytes 1048576 | tf_op jit(solution)/shard_map/all_to_all | solution.py:210
where the time goes:
time: 163 us; the launch traced here: 162 us
  Pallas kernels  68.1 us (42%)
  blocking collectives  41.1 us (25%)
  local copies, waits for them, and re-layouts  20 us (12%)
  waiting for transfers between devices  13.7 us (8%)
  other arithmetic  8.5 us (5%)
  matrix products  7.18 us (4%)
  starting transfers between devices  2.81 us (2%)
    pallas_call x1, Pallas kernels, point_part(): pl.pallas_call(point_kernel, grid=(rows // ROWS,), in_specs=[rowed, rowed...  53.3 us
    all_to_all x2, blocking collectives, to_owner(): lax.all_to_all(x, ('dp', 'slab'), split_axis=0, concat_axis=0, tiled=True)  41.1 us
    pallas_call x1, Pallas kernels, forward_modes(): pl.pallas_call(forward_kernel, grid=(chans // per,), in_specs=[pl.BlockSp...  14.9 us
    all_to_all x1, waiting for transfers between devices, from_owner(): lax.all_to_all(x, ('dp', 'slab'), split_axis=0, concat_axis=0, tiled=True)  13.7 us
    unnamed x15, local copies, waits for them, and re-layouts  5.91 us
    dot_general x1, matrix products, body(): grad = jnp.einsum('kjbri,kjbro->kjio', u, pair, precision=high)  5.84 us
    all_to_all x2, other arithmetic, to_owner(): lax.all_to_all(x, ('dp', 'slab'), split_axis=0, concat_axis=0, tiled=True)  3.87 us
  transfers between devices with their start and end apart: 1, of which 1 were waited for; matrix products, arithmetic and copies ran while one was open for 1% of the time, Pallas kernels for 0%

commit v1 on v0

--- a/solution.py
+++ b/solution.py
@@ -1,4 +1,3 @@
-import functools
 import math
 
 import jax
@@ -14,13 +13,14 @@
 NZ = 512
 KY = 32
 KZ = 32
+PAIRS = KY // 2
 ROWS = 16
 SUB = 8
 
-high = lax.Precision.HIGHEST
 gelu_coef = 0.7978845608028654
 cube_coef = 0.044715
 vmem_bytes = 56 * 1024 * 1024
+MESH = pl.DeviceIdType.MESH
 
 
 def halves(table):
@@ -35,7 +35,8 @@
 
 
 def y_table():
-    freq = np.concatenate([np.arange(KY // 2), np.arange(KY // 2) - KY // 2])
+    mode = np.concatenate([np.arange(0, KY, 2), np.arange(1, KY, 2)])
+    freq = np.where(mode < KY // 2, mode, mode - KY)
     angle = 2.0 * math.pi / NY * (np.outer(np.arange(NY), freq) % NY)
     return np.concatenate([np.cos(angle), np.sin(angle)], 1)
 
@@ -71,15 +72,267 @@
     w = first[:, : 2 * KZ] + first[:, 2 * KZ :] + both[2 * KY :, : 2 * KZ]
     real = w[:KY, :KZ] + w[KY:, KZ:]
     imag = w[:KY, KZ:] - w[KY:, :KZ]
-    return jnp.concatenate([real, imag], axis=1)
-
-
-def forward_kernel(x_ref, zt_ref, yt_ref, o_ref):
+    return jnp.concatenate([real[:PAIRS], imag[:PAIRS], real[PAIRS:], imag[PAIRS:]], axis=1)
+
+
+def halves_swapped(x):
+    half = x.shape[-1] // 2
+    return jnp.concatenate([x[:, half:], x[:, :half]], axis=1)
+
+
+class Links:
+    def __init__(self, dp, slab):
+        self.dp, self.slab = dp, slab
+        self.me_d, self.me_s = lax.axis_index("dp"), lax.axis_index("slab")
+        self.per_j, self.per_k = KY // dp, KZ // slab
+        self.owners = 2 // self.per_j
+
+    def greet(self):
+        barrier = pltpu.get_barrier_semaphore()
+
+        @pl.loop(1, self.dp)
+        def _(t):
+            there = lax.rem(self.me_d + t, self.dp)
+            pl.semaphore_signal(barrier, inc=1, device_id=(there, self.me_s), device_id_type=MESH)
+
+        for t in range(1, self.slab):
+            there = lax.rem(self.me_s + t, self.slab)
+            pl.semaphore_signal(barrier, inc=1, device_id=(self.me_d, there), device_id_type=MESH)
+
+    def greeted(self):
+        pl.semaphore_wait(pltpu.get_barrier_semaphore(), self.dp + self.slab - 2)
+
+    def copy(self, src, dst, send, recv, d, s):
+        return pltpu.make_async_remote_copy(
+            src_ref=src, dst_ref=dst, send_sem=send, recv_sem=recv,
+            device_id=(d, s), device_id_type=MESH,
+        )
+
+    def pack(self, modes, part, m):
+        chans = modes.shape[0] // PAIRS
+        turned = modes[pl.ds(m, chans, stride=PAIRS), :].T
+        for n in range(2):
+            own = turned[2 * n * KZ : 2 * (n + 1) * KZ]
+            rows = jnp.concatenate([own[:KZ], own[KZ:]], axis=1)
+            if self.per_j == 2:
+                d, place = m, n * self.per_k
+            else:
+                d, place = m * 2 + n, 0
+            for s in range(self.slab):
+                part[d, s, place : place + self.per_k, :] = rows[
+                    s * self.per_k : (s + 1) * self.per_k
+                ]
+
+    def to_owner(self, modes, part, near, total, got, sems):
+        near_send, near_recv, far_send, far_recv = sems
+        dp, slab, me_d, me_s = self.dp, self.slab, self.me_d, self.me_s
+        area = self.per_j * self.per_k
+
+        def near_copy(d, t):
+            there = lax.rem(me_s + t, slab)
+            return self.copy(
+                part.at[d, there], near.at[t - 1, d],
+                near_send.at[t - 1, d], near_recv.at[t - 1, d], me_d, there,
+            )
+
+        def far_copy(d):
+            return self.copy(
+                total.at[d], got.at[pl.ds(me_d * area, area)],
+                far_send.at[d], far_recv.at[me_d], d, me_s,
+            )
+
+        first = lax.div(lax.rem(me_d + 1, dp), self.owners)
+
+        @pl.loop(0, PAIRS)
+        def _(n):
+            m = lax.rem(first + n, PAIRS)
+            self.pack(modes, part, m)
+            for q in range(self.owners):
+                for t in range(1, slab):
+                    near_copy(m * self.owners + q, t).start()
+
+        def summed(d):
+            value = part[d, me_s]
+            for t in range(1, slab):
+                near_copy(d, t).wait_recv()
+                value = value + near[t - 1, d]
+            return value
+
+        @pl.loop(0, dp - 1)
+        def _(n):
+            d = lax.rem(me_d + 1 + n, dp)
+            total[d] = summed(d)
+            far_copy(d).start()
+
+        got[pl.ds(me_d * area, area), :] = summed(me_d)
+
+        @pl.loop(0, dp - 1)
+        def _(n):
+            src = lax.rem(me_d + dp - 1 - n, dp)
+            self.copy(
+                total.at[src], got.at[pl.ds(src * area, area)],
+                far_send.at[src], far_recv.at[src], src, me_s,
+            ).wait_recv()
+
+        @pl.loop(0, dp)
+        def _(d):
+            for t in range(1, slab):
+                near_copy(d, t).wait_send()
+
+        @pl.loop(0, dp - 1)
+        def _(n):
+            far_copy(lax.rem(me_d + 1 + n, dp)).wait_send()
+
+    def from_owner(self, values, back, spec, sems):
+        near_send, near_recv, far_send, far_recv = sems
+        dp, slab, me_d, me_s = self.dp, self.slab, self.me_d, self.me_s
+        area = self.per_j * self.per_k
+
+        def far_copy(d):
+            return self.copy(
+                values.at[pl.ds(d * area, area)], back.at[me_s, me_d],
+                far_send.at[d], far_recv.at[me_d], d, me_s,
+            )
+
+        def relay(d, t):
+            there = lax.rem(me_s + t, slab)
+            return self.copy(
+                back.at[me_s, d], back.at[me_s, d],
+                near_send.at[t - 1, d], near_recv.at[t - 1, d], me_d, there,
+            )
+
+        @pl.loop(0, dp - 1)
+        def _(n):
+            far_copy(lax.rem(me_d + 1 + n, dp)).start()
+
+        back[me_s, me_d] = values[pl.ds(me_d * area, area), :]
+        for t in range(1, slab):
+            relay(me_d, t).start()
+
+        @pl.loop(0, dp - 1)
+        def _(n):
+            src = lax.rem(me_d + dp - 1 - n, dp)
+            self.copy(
+                values.at[pl.ds(src * area, area)], back.at[me_s, src],
+                far_send.at[src], far_recv.at[src], src, me_s,
+            ).wait_recv()
+            for t in range(1, slab):
+                relay(src, t).start()
+
+        first = lax.div(me_d, self.owners)
+
+        @pl.loop(0, PAIRS)
+        def _(n):
+            m = lax.rem(first + PAIRS - n, PAIRS)
+            for q in range(self.owners):
+                d = m * self.owners + q
+                for t in range(1, slab):
+                    source = lax.rem(me_s + slab - t, slab)
+                    self.copy(
+                        back.at[source, d], back.at[source, d],
+                        near_send.at[t - 1, d], near_recv.at[t - 1, d], me_d, source,
+                    ).wait_recv()
+            self.unpack(back, spec, m)
+
+        @pl.loop(0, dp)
+        def _(d):
+            for t in range(1, slab):
+                relay(d, t).wait_send()
+
+        @pl.loop(0, dp - 1)
+        def _(n):
+            far_copy(lax.rem(me_d + 1 + n, dp)).wait_send()
+
+    def unpack(self, back, spec, m):
+        chans = spec.shape[0] // PAIRS
+        blocks = []
+        for n in range(2):
+            if self.per_j == 2:
+                d, place = m, n * self.per_k
+            else:
+                d, place = m * 2 + n, 0
+            rows = jnp.concatenate(
+                [back[s, d, place : place + self.per_k, :] for s in range(self.slab)], axis=0
+            )
+            blocks += [rows[:, :chans], rows[:, chans:]]
+        spec[pl.ds(m, chans, stride=PAIRS), :] = jnp.concatenate(blocks, axis=0).T
+
+
+def forward_kernel(
+    dp, slab, x_ref, zt_ref, yt_ref, w_ref, spec_ref, u_ref,
+    modes, part, near, total, got, mixer, values, back, *sems,
+):
+    links = Links(dp, slab)
+    step = pl.program_id(0)
     per, rows, length = x_ref.shape
+    chans = modes.shape[0] // PAIRS
+    area = links.per_j * links.per_k
+
+    @pl.when(step == 0)
+    def _():
+        links.greet()
+
     zval = mm(x_ref[...].reshape(per * rows, length), zt_ref[...])
     zval = (zval[:, : 2 * KZ] + zval[:, 2 * KZ :]).reshape(per, rows, 2 * KZ)
+    ytab = yt_ref[links.me_s]
     for c in range(per):
-        o_ref[c] = y_modes(zval[c], yt_ref[...])
+        place = pl.multiple_of((step * per + c) * PAIRS, PAIRS)
+        modes[pl.ds(place, PAIRS), :] = y_modes(zval[c], ytab)
+
+    @pl.when(step == pl.num_programs(0) - 1)
+    def _():
+        @pl.loop(0, area)
+        def _(r):
+            w = w_ref[lax.rem(r, links.per_k), lax.div(r, links.per_k)]
+            low = lax.broadcasted_iota(jnp.int32, w.shape, 1) < chans
+            turned = halves_swapped(w)
+            both = jnp.concatenate([w, jnp.where(low, -turned, turned)], axis=0)
+            top, rest = split(both)
+            mixer[r] = jnp.concatenate([top, rest], axis=1)
+
+        links.greeted()
+        links.to_owner(modes, part, near, total, got, sems[:4])
+        scale = 1.0 / math.sqrt(NY * NZ) / math.sqrt(KY * KZ)
+
+        @pl.loop(0, area)
+        def _(r):
+            u = got[pl.ds(r, dp, stride=area), :]
+            top, rest = split(u)
+            out = mm(jnp.concatenate([top, rest], axis=0), mixer[r])
+            wide = 2 * chans
+            v = out[:dp, :wide] + out[:dp, wide:] + out[dp:, :wide]
+            values[pl.ds(r, dp, stride=area), :] = v * scale
+
+        u_ref[...] = got[...]
+        links.from_owner(values, back, spec_ref, sems[4:])
+
+
+def grad_kernel(
+    dp, slab, g_ref, u_ref, grad_ref, part, near, total, got, left, *sems
+):
+    links = Links(dp, slab)
+    chans = g_ref.shape[0] // PAIRS
+    area = links.per_j * links.per_k
+    links.greet()
+
+    @pl.loop(0, area)
+    def _(r):
+        turned = u_ref[pl.ds(r, dp, stride=area), :].T
+        top, rest = split(jnp.concatenate([turned[:chans], turned[chans:]], axis=1))
+        left[r] = jnp.concatenate([top, top, rest], axis=1)
+
+    links.greeted()
+    links.to_owner(g_ref, part, near, total, got, sems)
+    scale = 1.0 / math.sqrt(NY * NZ) / math.sqrt(KY * KZ) / dp
+
+    @pl.loop(0, area)
+    def _(r):
+        g = got[pl.ds(r, dp, stride=area), :]
+        low = lax.broadcasted_iota(jnp.int32, g.shape, 1) < chans
+        turned = halves_swapped(g)
+        top, rest = split(jnp.concatenate([g, jnp.where(low, turned, -turned)], axis=0))
+        grad = mm(left[r], jnp.concatenate([top, rest, top], axis=0))
+        grad_ref[lax.rem(r, links.per_k), lax.div(r, links.per_k)] = grad * scale
 
 
 def point_kernel(
@@ -89,6 +342,7 @@
     step = pl.program_id(0)
     chans, rows = left.shape[:2]
     wide = 2 * KZ
+    me_s = lax.axis_index("slab")
 
     @pl.when(step == 0)
     def _():
@@ -102,12 +356,14 @@
             kron_ref[m * part : (m + 1) * part, :] = (
                 mm(rows_of, spread).astype(jnp.bfloat16) * same
             )
+        yback = yback_ref[me_s]
 
         def invert(o):
-            v = spec_ref[o]
+            pairs = spec_ref[pl.ds(pl.multiple_of(o * PAIRS, PAIRS), PAIRS), :]
+            v = jnp.concatenate([pairs[:, :wide], pairs[:, wide:]], axis=0)
             turned = jnp.concatenate([-v[:, KZ:], v[:, :KZ]], axis=1)
             top, rest = split(jnp.concatenate([v, turned], axis=0))
-            yval = mm(yback_ref[...], jnp.concatenate([top, rest, top], axis=0))
+            yval = mm(yback, jnp.concatenate([top, rest, top], axis=0))
             ytop, yrest = split(yval)
             b = bias_ref[o]
             b0 = b.astype(jnp.bfloat16).astype(jnp.float32)
@@ -145,8 +401,11 @@
 
     @pl.when(step == pl.num_programs(0) - 1)
     def _():
+        ytab = yt_ref[me_s]
+
         def forward(o):
-            g_ref[o] = y_modes(zsum[o], yt_ref[...])
+            place = pl.multiple_of(o * PAIRS, PAIRS)
+            g_ref[pl.ds(place, PAIRS), :] = y_modes(zsum[o], ytab)
 
         each(chans, forward)
 
@@ -155,21 +414,84 @@
     return pl.BlockSpec(shape, lambda i: (0,) * len(shape))
 
 
-def forward_modes(field, zt, yt):
+def link_scratch(dp, slab, chans):
+    area = (KY // dp) * (KZ // slab)
+    wide = 2 * chans
+    return [
+        pltpu.VMEM((dp, slab, area, wide), jnp.float32),
+        pltpu.VMEM((slab - 1, dp, area, wide), jnp.float32),
+        pltpu.VMEM((dp, area, wide), jnp.float32),
+        pltpu.VMEM((dp * area, wide), jnp.float32),
+    ]
+
+
+def link_sems(dp, slab):
+    return [
+        pltpu.SemaphoreType.DMA((slab - 1, dp)),
+        pltpu.SemaphoreType.DMA((slab - 1, dp)),
+        pltpu.SemaphoreType.DMA((dp,)),
+        pltpu.SemaphoreType.DMA((dp,)),
+    ]
+
+
+def forward_part(field, zt, yt, w_spec, dp, slab):
     chans, rows, length = field.shape
     per = 8
+    area = (KY // dp) * (KZ // slab)
+    wide = 2 * chans
+
+    def kernel(*refs):
+        forward_kernel(dp, slab, *refs)
+
     return pl.pallas_call(
-        forward_kernel,
+        kernel,
         grid=(chans // per,),
         in_specs=[
             pl.BlockSpec((per, rows, length), lambda i: (i, 0, 0)),
             whole(zt.shape),
             whole(yt.shape),
+            whole(w_spec.shape),
         ],
-        out_specs=pl.BlockSpec((per, KY, 2 * KZ), lambda i: (i, 0, 0)),
-        out_shape=jax.ShapeDtypeStruct((chans, KY, 2 * KZ), jnp.float32),
-        compiler_params=pltpu.CompilerParams(vmem_limit_bytes=vmem_bytes),
-    )(field, zt, yt)
+        out_specs=[whole((chans * PAIRS, 4 * KZ)), whole((dp * area, wide))],
+        out_shape=[
+            jax.ShapeDtypeStruct((chans * PAIRS, 4 * KZ), jnp.float32),
+            jax.ShapeDtypeStruct((dp * area, wide), jnp.float32),
+        ],
+        scratch_shapes=[pltpu.VMEM((chans * PAIRS, 4 * KZ), jnp.float32)]
+        + link_scratch(dp, slab, chans)
+        + [
+            pltpu.VMEM((area, wide, 2 * wide), jnp.bfloat16),
+            pltpu.VMEM((dp * area, wide), jnp.float32),
+            pltpu.VMEM((slab, dp, area, wide), jnp.float32),
+        ]
+        + link_sems(dp, slab)
+        + link_sems(dp, slab),
+        compiler_params=pltpu.CompilerParams(
+            vmem_limit_bytes=vmem_bytes, collective_id=0, has_side_effects=True
+        ),
+    )(field, zt, yt, w_spec)
+
+
+def grad_part(gmodes, u, dp, slab):
+    chans = gmodes.shape[0] // PAIRS
+    per_j, per_k = KY // dp, KZ // slab
+    inside = pl.BlockSpec(memory_space=pltpu.VMEM)
+
+    def kernel(*refs):
+        grad_kernel(dp, slab, *refs)
+
+    return pl.pallas_call(
+        kernel,
+        in_specs=[inside, inside],
+        out_specs=inside,
+        out_shape=jax.ShapeDtypeStruct((per_k, per_j, chans, 2 * chans), jnp.float32),
+        scratch_shapes=link_scratch(dp, slab, chans)
+        + [pltpu.VMEM((per_j * per_k, chans, 6 * dp), jnp.bfloat16)]
+        + link_sems(dp, slab),
+        compiler_params=pltpu.CompilerParams(
+            vmem_limit_bytes=vmem_bytes, collective_id=1, has_side_effects=True
+        ),
+    )(gmodes, u)
 
 
 def point_part(field, cot, spec, bias, skip, zt, yt, back, yback):
@@ -180,10 +502,10 @@
         grid=(rows // ROWS,),
         in_specs=[rowed, rowed]
         + [whole(a.shape) for a in (spec, bias, skip, zt, yt, back, yback)],
-        out_specs=[rowed, whole((chans, KY, 2 * KZ))],
+        out_specs=[rowed, whole((chans * PAIRS, 4 * KZ))],
         out_shape=[
             jax.ShapeDtypeStruct(field.shape, jnp.bfloat16),
-            jax.ShapeDtypeStruct((chans, KY, 2 * KZ), jnp.float32),
+            jax.ShapeDtypeStruct((chans * PAIRS, 4 * KZ), jnp.float32),
         ],
         scratch_shapes=[
             pltpu.VMEM((chans, rows, 8 * KZ), jnp.bfloat16),
@@ -194,57 +516,28 @@
     )(field, cot, spec, bias, skip, zt, yt, back, yback)
 
 
-def to_owner(modes, dp, slab):
-    chans = modes.shape[0]
-    x = modes.reshape(chans, dp, KY // dp, 2, slab, KZ // slab)
-    x = x.transpose(1, 4, 5, 2, 3, 0).reshape(dp * slab, -1, chans)
-    x = lax.all_to_all(x, ("dp", "slab"), split_axis=0, concat_axis=0, tiled=True)
-    x = x.reshape(dp, slab, KZ // slab, KY // dp, 2, chans).sum(1)
-    return x.transpose(1, 2, 0, 3, 4)
-
-
-def from_owner(spec, dp, slab):
-    chans = spec.shape[-1]
-    x = spec.transpose(2, 0, 1, 3, 4).reshape(dp, 1, -1, chans)
-    x = jnp.broadcast_to(x, (dp, slab) + x.shape[2:]).reshape(dp * slab, -1, chans)
-    x = lax.all_to_all(x, ("dp", "slab"), split_axis=0, concat_axis=0, tiled=True)
-    x = x.reshape(dp, slab, KZ // slab, KY // dp, 2, chans)
-    return x.transpose(5, 0, 3, 4, 1, 2).reshape(chans, KY, 2 * KZ)
-
-
 def body(snapshots, cotangent, w_spec, first_moment, second_moment, w_skip, bias):
     chans, rows, length = snapshots.shape[1:]
-    spec_scale = 1.0 / math.sqrt(NY * NZ)
-    out_scale = 1.0 / math.sqrt(KY * KZ)
     dp = lax.axis_size("dp")
     slab = lax.axis_size("slab")
-    start = lax.axis_index("slab") * rows
     ztop, zrest = halves(z_table())
     ytop, yrest = halves(y_table())
     zt = jnp.asarray(np.concatenate([ztop, zrest], 1))
     ones = np.zeros((2 * KZ, length), ml_dtypes.bfloat16)
     ones[:3] = 1
     back = jnp.asarray(np.concatenate([ztop.T, ztop.T, zrest.T, ones], 0))
-    yt = jnp.asarray(np.concatenate([ytop, yrest], 1).T)
-    yt = lax.dynamic_slice_in_dim(yt, start, rows, 1)
-    yback = jnp.asarray(np.concatenate([ytop, ytop, yrest], 1))
-    yback = lax.dynamic_slice_in_dim(yback, start, rows, 0)
+    yt = np.concatenate([ytop, yrest], 1).reshape(slab, rows, -1)
+    yt = jnp.asarray(np.ascontiguousarray(yt.transpose(0, 2, 1)))
+    yback = jnp.asarray(np.concatenate([ytop, ytop, yrest], 1).reshape(slab, rows, -1))
     bias_lanes = jnp.pad(
         jnp.broadcast_to(bias[:, None, None], (chans, 1, 3)), ((0, 0), (0, 0), (0, 2 * KZ - 3))
     )
 
-    u = to_owner(forward_modes(snapshots[0], zt, yt), dp, slab) * spec_scale
-    prod = jnp.einsum("kjbri,kjio->kjbro", u, w_spec, precision=high)
-    vreal = prod[..., 0, :chans] - prod[..., 1, chans:]
-    vimag = prod[..., 0, chans:] + prod[..., 1, :chans]
-    spec = from_owner(jnp.stack([vreal, vimag], 3) * out_scale, dp, slab)
+    spec, u = forward_part(snapshots[0], zt, yt, w_spec, dp, slab)
     layer_out, gmodes = point_part(
         snapshots[0], cotangent[0], spec, bias_lanes, w_skip.T, zt, yt, back, yback
     )
-    g = to_owner(gmodes, dp, slab) * (out_scale / dp)
-    turned = jnp.stack([g[..., 1, :], -g[..., 0, :]], 3)
-    pair = jnp.concatenate([g, turned], -1)
-    grad = jnp.einsum("kjbri,kjbro->kjio", u, pair, precision=high)
+    grad = grad_part(gmodes, u, dp, slab)
     new_first = 0.9 * first_moment + 0.1 * grad
     new_second = 0.95 * second_moment + 0.05 * grad * grad
     bias_first = 1.0 - 0.9**10

time: 163 us -> 142 us (0.87)
  Pallas kernels: 68.1 us -> 134 us
  blocking collectives: 41.1 us -> 0 us
  local copies, waits for them, and re-layouts: 20 us -> 2.85 us
  waiting for transfers between devices: 13.7 us -> 0 us
  matrix products: 7.18 us -> 0 us
  other arithmetic: 8.5 us -> 3.51 us
  starting transfers between devices: 2.81 us -> 0 us
    pallas_call x1 -> x2, Pallas kernels: 14.9 us -> 79.4 us  [the longest x1 50.3 us: forward_part(): pl.pallas_call(kernel, grid=(chans // per,), in_specs=[pl.BlockSpec((per,...]
    all_to_all x2 -> x0, blocking collectives: 41.1 us -> none  [to_owner(): lax.all_to_all(x, ('dp', 'slab'), split_axis=0, concat_axis=0, tiled=True)]
    all_to_all x1 -> x0, waiting for transfers between devices: 13.7 us -> none  [from_owner(): lax.all_to_all(x, ('dp', 'slab'), split_axis=0, concat_axis=0, tiled=True)]
    dot_general x2 -> x0, matrix products: 7.18 us -> none  [the longest x1 5.84 us: body(): grad = jnp.einsum('kjbri,kjbro->kjio', u, pair, precision=high)]
    all_to_all x3 -> x0, other arithmetic: 5.81 us -> none  [the longest x2 3.87 us: to_owner(): lax.all_to_all(x, ('dp', 'slab'), split_axis=0, concat_axis=0, tiled=True)]
    unnamed x15 -> x7, local copies, waits for them, and re-layouts: 5.91 us -> 1.43 us
    transpose x3 -> x0, local copies, waits for them, and re-layouts: 3.72 us -> none  [the longest x2 2.6 us: to_owner(): x = x.transpose(1, 4, 5, 2, 3, 0).reshape(dp * slab, -1, chans)]
    pallas_call x2 -> x0, local copies, waits for them, and re-layouts: 3.54 us -> none  [the longest x1 1.77 us: point_part(): pl.pallas_call(point_kernel, grid=(rows // ROWS,), in_specs=[rowed, rowed...]
  transfers between devices with their start and end apart: 1 -> 0, of which waited for: 1 -> 0; matrix products, arithmetic and copies ran while one was open for 1% -> 0% of each run, Pallas kernels for 0% -> 0%
where the time goes in v1:
time: 142 us; the launch traced here: 141 us
  Pallas kernels  134 us (94%)
  other arithmetic  3.51 us (2%)
  local copies, waits for them, and re-layouts  2.85 us (2%)
    pallas_call x1, Pallas kernels, point_part(): pl.pallas_call(point_kernel, grid=(rows // ROWS,), in_specs=[rowed, rowed...  54.7 us
    pallas_call x1, Pallas kernels, forward_part(): pl.pallas_call(kernel, grid=(chans // per,), in_specs=[pl.BlockSpec((per,...  50.3 us
    pallas_call x1, Pallas kernels, grad_part(): pl.pallas_call(kernel, in_specs=[inside, inside], out_specs=inside, out_s...  29.1 us
    sub x1, other arithmetic, body(): w_spec - 0.01 * (new_first / bias_first) / (jnp.sqrt(new_second / bias_se...  3.51 us

profile of v1, /device:TPU:1, one launch (start us, length us, event | category | flops | bytes accessed | tf_op | source)
XLA Modules:
  0.0 141.1 jit_solution(16194625959422167130)
XLA Ops:
  0.6 1.4 copy.15
  2.0 0.8 broadcast_in_dim.4
  2.8 0.6 pad.4.bias_ref
  3.5 50.3 %shard_map.138 = (f32[1024,128]{1,0:T(8,128)}, f32[512,128]{1,0:T(8,128)}) custom-call(bf16[64,256,512]{2,1,0:T(8,128)(2,1)} %bitcast.4, bf16[512,128]{1,0:T(8,128)(2,1)} %constant.29.clone.refs_1_.zt_ref, bf16[2,128,256]{2,1,0:T(8,128)(2,1)} %constant.31.clone.refs_2_.yt_ref, f32[16,2,64,128]{3,2,1,0:T(8,128)} %refs_3_.1), custom_call_target="tpu_custom_call" | custom-call | tf_op jit(solution)/shard_map/pallas_call | solution.py:446
  53.8 0.0 copy-start
  53.8 0.0 copy-start.1
  53.8 0.0 copy-start.2
  53.8 54.7 %shard_map.139 = (bf16[64,256,512]{2,1,0:T(8,128)(2,1)}, f32[1024,128]{1,0:T(8,128)}) custom-call(bf16[64,256,512]{2,1,0:T(8,128)(2,1)} %bitcast.5, bf16[64,256,512]{2,1,0:T(8,128)(2,1)} %bitcast.6, f32[1024,128]{1,0:T(8,128)} %get-tuple-element.8.spec_ref, f32[64,1,64]{2,1,0:T(1,128)} %pad.4.bias_ref, bf16[64,64]{1,0:T(8,128)(2,1)} %bitcast.7, ...), custom_call_target="tpu_custom_call" | custom-call | tf_op jit(solution)/shard_map/pallas_call | solution.py:500
  108.5 29.1 %shard_map.140 = f32[16,2,64,128]{3,2,1,0:T(8,128)} custom-call(f32[1024,128]{1,0:T(8,128)} %get-tuple-element.10.refs_0_, f32[512,128]{1,0:T(8,128)} %get-tuple-element.11.refs_1_), custom_call_target="tpu_custom_call" | custom-call | tf_op jit(solution)/shard_map/pallas_call | solution.py:483
  137.6 0.0 copy-done
  137.6 0.0 copy-done.1
  137.6 0.0 copy-done.2
  137.6 3.5 %divide_subtract_fusion = (f32[16,2,64,128]{3,2,1,0:T(8,128)}, f32[16,2,64,128]{3,2,1,0:T(8,128)}, f32[16,2,64,128]{3,2,1,0:T(8,128)}) fusion(f32[16,2,64,128]{3,2,1,0:T(8,128)S(1)} %copy-done, f32[16,2,64,128]{3,2,1,0:T(8,128)} %shard_map.140, f32[16,2,64,128]{3,2,1,0:T(8,128)S(1)} %copy-done.1, f32[16,2,64,128]{3,2,1,0:T(8,128)S(1)} %copy-done.2), kind=kLoop, calls=%fused_computation.2 | loop fusion | flops 3145728 | bytes 7340032 | tf_op jit(solution)/shard_map/sub | solution.py:545
Async XLA Ops:
  53.8 83.8 %copy-start = (f32[16,2,64,128]{3,2,1,0:T(8,128)S(1)}, f32[16,2,64,128]{3,2,1,0:T(8,128)}, u32[]{:S(2)}) copy-start(f32[16,2,64,128]{3,2,1,0:T(8,128)} %refs_3_.1) | copy-start | bytes 3145732
  53.8 83.8 %copy-start.1 = (f32[16,2,64,128]{3,2,1,0:T(8,128)S(1)}, f32[16,2,64,128]{3,2,1,0:T(8,128)}, u32[]{:S(2)}) copy-start(f32[16,2,64,128]{3,2,1,0:T(8,128)} %param.14) | copy-start | bytes 3145732
  53.8 83.8 %copy-start.2 = (f32[16,2,64,128]{3,2,1,0:T(8,128)S(1)}, f32[16,2,64,128]{3,2,1,0:T(8,128)}, u32[]{:S(2)}) copy-start(f32[16,2,64,128]{3,2,1,0:T(8,128)} %param.15) | copy-start | bytes 3145732

commit v2 on v1

v2 whole, which is shorter than its diff:
```python
import math

import jax
import jax.numpy as jnp
import ml_dtypes
import numpy as np
from jax import lax
from jax.experimental import pallas as pl
from jax.experimental.pallas import tpu as pltpu
from jax.sharding import PartitionSpec as P

NY = 512
NZ = 512
KY = 32
KZ = 32
PAIRS = KY // 2
ROWS = 16
SUB = 8

gelu_coef = 0.7978845608028654
cube_coef = 0.044715
vmem_bytes = 56 * 1024 * 1024
MESH = pl.DeviceIdType.MESH


def halves(table):
    top = table.astype(ml_dtypes.bfloat16)
    rest = (table - top.astype(np.float64)).astype(ml_dtypes.bfloat16)
    return top, rest


def z_table():
    angle = 2.0 * math.pi / NZ * (np.outer(np.arange(NZ), np.arange(KZ)) % NZ)
    return np.concatenate([np.cos(angle), -np.sin(angle)], 1)


def y_table(mode):
    freq = np.where(mode < KY // 2, mode, mode - KY)
    angle = 2.0 * math.pi / NY * (np.outer(np.arange(NY), freq) % NY)
    return np.concatenate([np.cos(angle), np.sin(angle)], 1)


def split(x):
    top = x.astype(jnp.bfloat16)
    return top, (x - top.astype(jnp.float32)).astype(jnp.bfloat16)


def mm(a, b):
    return jnp.dot(a, b, preferred_element_type=jnp.float32)


def one_hot(shape, test):
    rows = lax.broadcasted_iota(jnp.int32, shape, 0)
    columns = lax.broadcasted_iota(jnp.int32, shape, 1)
    return jnp.where(test(rows, columns), 1.0, 0.0).astype(jnp.bfloat16)


def each(count, step):
    per = math.gcd(count, 8)

    @pl.loop(0, count // per)
    def _(i):
        for n in range(per):
            step(i * per + n)


def halves_swapped(x):
    half = x.shape[-1] // 2
    return jnp.concatenate([x[:, half:], x[:, :half]], axis=1)


def y_modes(both, ytab, slab):
    both = mm(ytab, both)
    first = both[: 2 * KY]
    w = first[:, : 2 * KZ] + first[:, 2 * KZ :] + both[2 * KY :, : 2 * KZ]
    per_k = KZ // slab
    group = 64 // per_k
    count = KY // group
    lane = lax.broadcasted_iota(jnp.int32, (KY, 2 * KZ), 1)
    real = lane % (2 * per_k) < per_k
    sine = w[KY:]
    ahead = jnp.concatenate([sine[:, per_k:], sine[:, :per_k]], axis=1)
    behind = jnp.concatenate([sine[:, 2 * KZ - per_k :], sine[:, : 2 * KZ - per_k]], axis=1)
    out = w[:KY] + jnp.where(real, ahead, -behind)
    return [
        jnp.concatenate(
            [
                out[g * count : (g + 1) * count, s * 2 * per_k : (s + 1) * 2 * per_k]
                for g in range(group)
            ],
            axis=1,
        )
        for s in range(slab)
    ]


class Links:
    def __init__(self, dp, slab):
        self.dp, self.slab = dp, slab
        self.me_d, self.me_s = lax.axis_index("dp"), lax.axis_index("slab")
        self.per_j, self.per_k = KY // dp, KZ // slab
        self.area = self.per_j * self.per_k
        self.group = 64 // self.per_k
        self.count = KY // self.group

    def greet(self):
        barrier = pltpu.get_barrier_semaphore()

        @pl.loop(1, self.dp)
        def _(t):
            there = lax.rem(self.me_d + t, self.dp)
            pl.semaphore_signal(barrier, inc=1, device_id=(there, self.me_s), device_id_type=MESH)

        for t in range(1, self.slab):
            there = lax.rem(self.me_s + t, self.slab)
            pl.semaphore_signal(barrier, inc=1, device_id=(self.me_d, there), device_id_type=MESH)

    def greeted(self):
        pl.semaphore_wait(pltpu.get_barrier_semaphore(), self.dp + self.slab - 2)

    def copy(self, src, dst, send, recv, d, s):
        return pltpu.make_async_remote_copy(
            src_ref=src, dst_ref=dst, send_sem=send, recv_sem=recv,
            device_id=(d, s), device_id_type=MESH,
        )

    def near_copy(self, step, rows, part, near, sems, t):
        there = lax.rem(self.me_s + t, self.slab)
        own = pl.ds(pl.multiple_of(step * rows, rows), rows)
        return self.copy(
            part.at[there, own], near.at[t - 1, own],
            sems[0].at[t - 1, step], sems[1].at[t - 1, step], self.me_d, there,
        )

    def chunk(self, step, per, halves_of, ytab, part, near, sems):
        rows = per * self.count
        start = pl.multiple_of(step * rows, rows)
        for c in range(per):
            for s, value in enumerate(y_modes(halves_of(c), ytab, self.slab)):
                part[s, pl.ds(start + c * self.count, self.count), :] = value

        @pl.when(step == 0)
        def _():
            self.greeted()

        for t in range(1, self.slab):
            self.near_copy(step, rows, part, near, sems, t).start()

    def to_owner(self, steps, part, near, total, got, sems):
        far_send, far_recv = sems[2:]
        dp, slab, me_d, me_s, area = self.dp, self.slab, self.me_d, self.me_s, self.area
        rows = part.shape[1] // steps
        chans = part.shape[1] // self.count

        @pl.loop(0, steps)
        def _(step):
            for t in range(1, slab):
                self.near_copy(step, rows, part, near, sems, t).wait_recv()

        def far_copy(d):
            return self.copy(
                total.at[d], got.at[pl.ds(me_d * area, area)],
                far_send.at[d], far_recv.at[me_d], d, me_s,
            )

        owners = self.group // self.per_j
        first = lax.div(lax.rem(me_d + 1, dp), owners)

        @pl.loop(0, self.count)
        def _(n):
            q = lax.rem(first + n, self.count)
            own = pl.ds(q, chans, stride=self.count)
            value = part[me_s, own, :]
            for t in range(1, slab):
                value = value + near[t - 1, own, :]
            turned = value.T
            for g in range(self.group):
                block = turned[2 * g * self.per_k : 2 * (g + 1) * self.per_k]
                place = (g % self.per_j) * self.per_k
                d = q * owners + g // self.per_j
                total[d, place : place + self.per_k, :] = jnp.concatenate(
                    [block[: self.per_k], block[self.per_k :]], axis=1
                )
            for g in range(owners):
                d = q * owners + g

                @pl.when(d != me_d)
                def _():
                    far_copy(d).start()

        got[pl.ds(me_d * area, area), :] = total[me_d]

        @pl.loop(0, dp - 1)
        def _(n):
            src = lax.rem(me_d + dp - 1 - n, dp)
            self.copy(
                total.at[src], got.at[pl.ds(src * area, area)],
                far_send.at[src], far_recv.at[src], src, me_s,
            ).wait_recv()

        @pl.loop(0, steps)
        def _(step):
            for t in range(1, slab):
                self.near_copy(step, rows, part, near, sems, t).wait_send()

        @pl.loop(0, dp - 1)
        def _(n):
            far_copy(lax.rem(me_d + 1 + n, dp)).wait_send()

    def from_owner(self, values, back, spec, sems):
        near_send, near_recv, far_send, far_recv = sems
        dp, slab, me_d, me_s, area = self.dp, self.slab, self.me_d, self.me_s, self.area

        def far_copy(d):
            return self.copy(
                values.at[pl.ds(d * area, area)], back.at[me_s, me_d],
                far_send.at[d], far_recv.at[me_d], d, me_s,
            )

        def relay(d, t):
            there = lax.rem(me_s + t, slab)
            return self.copy(
                back.at[me_s, d], back.at[me_s, d],
                near_send.at[t - 1, d], near_recv.at[t - 1, d], me_d, there,
            )

        @pl.loop(0, dp - 1)
        def _(n):
            far_copy(lax.rem(me_d + 1 + n, dp)).start()

        back[me_s, me_d] = values[pl.ds(me_d * area, area), :]
        for t in range(1, slab):
            relay(me_d, t).start()

        @pl.loop(0, dp - 1)
        def _(n):
            src = lax.rem(me_d + dp - 1 - n, dp)
            self.copy(
                values.at[pl.ds(src * area, area)], back.at[me_s, src],
                far_send.at[src], far_recv.at[src], src, me_s,
            ).wait_recv()
            for t in range(1, slab):
                relay(src, t).start()

        owners = 2 // self.per_j
        first = lax.div(me_d, owners)

        @pl.loop(0, PAIRS)
        def _(n):
            m = lax.rem(first + PAIRS - n, PAIRS)
            for q in range(owners):
                d = m * owners + q
                for t in range(1, slab):
                    source = lax.rem(me_s + slab - t, slab)
                    self.copy(
                        back.at[source, d], back.at[source, d],
                        near_send.at[t - 1, d], near_recv.at[t - 1, d], me_d, source,
                    ).wait_recv()
            self.unpack(back, spec, m)

        @pl.loop(0, dp)
        def _(d):
            for t in range(1, slab):
                relay(d, t).wait_send()

        @pl.loop(0, dp - 1)
        def _(n):
            far_copy(lax.rem(me_d + 1 + n, dp)).wait_send()

    def unpack(self, back, spec, m):
        chans = spec.shape[0] // PAIRS
        blocks = []
        for n in range(2):
            if self.per_j == 2:
                d, place = m, n * self.per_k
            else:
                d, place = m * 2 + n, 0
            rows = jnp.concatenate(
                [back[s, d, place : place + self.per_k, :] for s in range(self.slab)], axis=0
            )
            blocks += [rows[:, :chans], rows[:, chans:]]
        spec[pl.ds(m, chans, stride=PAIRS), :] = jnp.concatenate(blocks, axis=0).T


def forward_kernel(
    dp, slab, x_ref, zt_ref, yt_ref, w_ref, spec_ref, u_ref,
    part, near, total, got, mixer, values, back, *sems,
):
    links = Links(dp, slab)
    step = pl.program_id(0)
    per, rows, length = x_ref.shape
    chans = part.shape[1] // links.count
    area = links.area
    steps = chans // per

    @pl.when(step == 0)
    def _():
        links.greet()

    zval = mm(x_ref[...].reshape(per * rows, length), zt_ref[...])
    zval = (zval[:, : 2 * KZ] + zval[:, 2 * KZ :]).reshape(per, rows, 2 * KZ)

    def halves_of(c):
        return jnp.concatenate(split(zval[c]), axis=1)

    links.chunk(step, per, halves_of, yt_ref[links.me_s], part, near, sems[:4])

    @pl.when(step == pl.num_programs(0) - 1)
    def _():
        def prepare(r):
            w = w_ref[lax.rem(r, links.per_k), lax.div(r, links.per_k)]
            low = lax.broadcasted_iota(jnp.int32, w.shape, 1) < chans
            turned = halves_swapped(w)
            both = jnp.concatenate([w, jnp.where(low, -turned, turned)], axis=0)
            top, rest = split(both)
            mixer[r] = jnp.concatenate([top, rest], axis=1)

        each(area, prepare)
        links.to_owner(steps, part, near, total, got, sems[:4])
        scale = 1.0 / math.sqrt(NY * NZ) / math.sqrt(KY * KZ)

        def mix(r):
            u = got[pl.ds(r, dp, stride=area), :]
            top, rest = split(u)
            out = mm(jnp.concatenate([top, rest], axis=0), mixer[r])
            wide = 2 * chans
            v = out[:dp, :wide] + out[:dp, wide:] + out[dp:, :wide]
            values[pl.ds(r, dp, stride=area), :] = v * scale

        each(area, mix)
        u_ref[...] = got[...]
        links.from_owner(values, back, spec_ref, sems[4:])


def grad_kernel(
    dp, slab, z_ref, yt_ref, u_ref, grad_ref, part, near, total, got, left, *sems
):
    links = Links(dp, slab)
    step = pl.program_id(0)
    per = z_ref.shape[0]
    chans = part.shape[1] // links.count
    area = links.area
    steps = chans // per

    @pl.when(step == 0)
    def _():
        links.greet()

    links.chunk(step, per, lambda c: z_ref[c], yt_ref[links.me_s], part, near, sems)

    @pl.when(step == pl.num_programs(0) - 1)
    def _():
        def prepare(r):
            turned = u_ref[pl.ds(r, dp, stride=area), :].T
            top, rest = split(jnp.concatenate([turned[:chans], turned[chans:]], axis=1))
            left[r] = jnp.concatenate([top, top, rest], axis=1)

        each(area, prepare)
        links.to_owner(steps, part, near, total, got, sems)
        scale = 1.0 / math.sqrt(NY * NZ) / math.sqrt(KY * KZ) / dp

        def multiply(r):
            g = got[pl.ds(r, dp, stride=area), :]
            low = lax.broadcasted_iota(jnp.int32, g.shape, 1) < chans
            turned = halves_swapped(g)
            top, rest = split(jnp.concatenate([g, jnp.where(low, turned, -turned)], axis=0))
            grad = mm(left[r], jnp.concatenate([top, rest, top], axis=0))
            grad_ref[lax.rem(r, links.per_k), lax.div(r, links.per_k)] = grad * scale

        each(area, multiply)


def point_kernel(
    x_ref, cot_ref, spec_ref, bias_ref, skip_ref, zt_ref, back_ref, yback_ref,
    out_ref, z_ref, left, kron_ref,
):
    step = pl.program_id(0)
    chans, rows = left.shape[:2]
    wide = 2 * KZ
    me_s = lax.axis_index("slab")

    @pl.when(step == 0)
    def _():
        tall = chans * SUB
        part = tall // 4
        spread = one_hot((chans, tall), lambda i, r: i == r // SUB)
        for m in range(4):
            pick = one_hot((part, chans), lambda r, o: (r + m * part) // SUB == o)
            rows_of = lax.dot_general(
                pick, skip_ref[...], (((1,), (1,)), ((), ())), preferred_element_type=jnp.float32
            ).astype(jnp.bfloat16)
            same = one_hot((part, tall), lambda r, s: r % SUB == s % SUB)
            kron_ref[m * part : (m + 1) * part, :] = (
                mm(rows_of, spread).astype(jnp.bfloat16) * same
            )
        yback = yback_ref[me_s]

        def invert(o):
            pairs = spec_ref[pl.ds(pl.multiple_of(o * PAIRS, PAIRS), PAIRS), :]
            v = jnp.concatenate([pairs[:, :wide], pairs[:, wide:]], axis=0)
            turned = jnp.concatenate([-v[:, KZ:], v[:, :KZ]], axis=1)
            top, rest = split(jnp.concatenate([v, turned], axis=0))
            yval = mm(yback, jnp.concatenate([top, rest, top], axis=0))
            ytop, yrest = split(yval)
            b = jnp.full((1, wide), bias_ref[o], jnp.float32)
            b0 = b.astype(jnp.bfloat16).astype(jnp.float32)
            b1 = (b - b0).astype(jnp.bfloat16).astype(jnp.float32)
            lane = lax.broadcasted_iota(jnp.int32, b.shape, 1)
            terms = jnp.where(lane == 0, b0, jnp.where(lane == 1, b1, b - b0 - b1))
            terms = jnp.broadcast_to(terms, (rows, wide)).astype(jnp.bfloat16)
            left[o] = jnp.concatenate([ytop, yrest, ytop, terms], axis=1)

        each(chans, invert)

    here = pl.ds(pl.multiple_of(step * ROWS, ROWS), ROWS)
    field = x_ref[...].astype(jnp.float32)
    terms = left[:, here, :].astype(jnp.float32)
    values, sums = [], []
    for m in range(ROWS // SUB):
        own = slice(m * SUB, (m + 1) * SUB)
        x = field[:, own].reshape(chans * SUB, NZ).astype(jnp.bfloat16)
        term = terms[:, own].reshape(chans * SUB, 4 * wide).astype(jnp.bfloat16)
        pre = mm(kron_ref[...], x) + mm(term, back_ref[...])
        sq = pre * pre
        t = jnp.tanh(pre * (gelu_coef + (gelu_coef * cube_coef) * sq))
        h = 0.5 + 0.5 * t
        value = pre * h
        values.append(value.reshape(chans, SUB, NZ))
        grow = 2.0 * gelu_coef + (6.0 * gelu_coef * cube_coef) * sq
        cot = cot_ref[...].astype(jnp.float32)[:, own].reshape(chans * SUB, NZ)
        slope = cot * (h + value * (0.5 - 0.5 * t) * grow)
        top, rest = split(slope)
        zval = mm(top, zt_ref[...])
        zval = zval[:, :wide] + zval[:, wide:] + mm(rest, zt_ref[:, :wide])
        sums.append(zval.reshape(chans, SUB, wide))
    out_ref[...] = jnp.concatenate(values, axis=1).astype(jnp.bfloat16)
    z_ref[...] = jnp.concatenate(split(jnp.concatenate(sums, axis=1)), axis=2)


def whole(shape):
    return pl.BlockSpec(shape, lambda i: (0,) * len(shape))


def link_scratch(dp, slab, chans):
    area = (KY // dp) * (KZ // slab)
    rows = chans * KY * (KZ // slab) // 64
    wide = 2 * chans
    return [
        pltpu.VMEM((slab, rows, 128), jnp.float32),
        pltpu.VMEM((slab - 1, rows, 128), jnp.float32),
        pltpu.VMEM((dp, area, wide), jnp.float32),
        pltpu.VMEM((dp * area, wide), jnp.float32),
    ]


def link_sems(dp, slab, steps):
    return [
        pltpu.SemaphoreType.DMA((slab - 1, steps)),
        pltpu.SemaphoreType.DMA((slab - 1, steps)),
        pltpu.SemaphoreType.DMA((dp,)),
        pltpu.SemaphoreType.DMA((dp,)),
    ]


def forward_part(field, zt, yt, w_spec, dp, slab):
    chans, rows, length = field.shape
    per = 8
    area = (KY // dp) * (KZ // slab)
    wide = 2 * chans

    def kernel(*refs):
        forward_kernel(dp, slab, *refs)

    return pl.pallas_call(
        kernel,
        grid=(chans // per,),
        in_specs=[
            pl.BlockSpec((per, rows, length), lambda i: (i, 0, 0)),
            whole(zt.shape),
            whole(yt.shape),
            whole(w_spec.shape),
        ],
        out_specs=[whole((chans * PAIRS, 4 * KZ)), whole((dp * area, wide))],
        out_shape=[
            jax.ShapeDtypeStruct((chans * PAIRS, 4 * KZ), jnp.float32),
            jax.ShapeDtypeStruct((dp * area, wide), jnp.float32),
        ],
        scratch_shapes=link_scratch(dp, slab, chans)
        + [
            pltpu.VMEM((area, wide, 2 * wide), jnp.bfloat16),
            pltpu.VMEM((dp * area, wide), jnp.float32),
            pltpu.VMEM((slab, dp, area, wide), jnp.float32),
        ]
        + link_sems(dp, slab, chans // per)
        + link_sems(dp, slab, dp),
        compiler_params=pltpu.CompilerParams(
            vmem_limit_bytes=vmem_bytes, collective_id=0, has_side_effects=True
        ),
    )(field, zt, yt, w_spec)


def grad_part(zsum, yt, u, dp, slab):
    chans, rows, width = zsum.shape
    per = 8
    per_j, per_k = KY // dp, KZ // slab

    def kernel(*refs):
        grad_kernel(dp, slab, *refs)

    return pl.pallas_call(
        kernel,
        grid=(chans // per,),
        in_specs=[
            pl.BlockSpec((per, rows, width), lambda i: (i, 0, 0)),
            whole(yt.shape),
            whole(u.shape),
        ],
        out_specs=whole((per_k, per_j, chans, 2 * chans)),
        out_shape=jax.ShapeDtypeStruct((per_k, per_j, chans, 2 * chans), jnp.float32),
        scratch_shapes=link_scratch(dp, slab, chans)
        + [pltpu.VMEM((per_j * per_k, chans, 6 * dp), jnp.bfloat16)]
        + link_sems(dp, slab, chans // per),
        compiler_params=pltpu.CompilerParams(
            vmem_limit_bytes=vmem_bytes, collective_id=1, has_side_effects=True
        ),
    )(zsum, yt, u)


def point_part(field, cot, spec, bias, skip, zt, back, yback):
    chans, rows, length = field.shape
    rowed = pl.BlockSpec((chans, ROWS, length), lambda i: (0, i, 0))
    return pl.pallas_call(
        point_kernel,
        grid=(rows // ROWS,),
        in_specs=[rowed, rowed, whole(spec.shape), pl.BlockSpec(memory_space=pltpu.SMEM)]
        + [whole(a.shape) for a in (skip, zt, back, yback)],
        out_specs=[rowed, pl.BlockSpec((chans, ROWS, 4 * KZ), lambda i: (0, i, 0))],
        out_shape=[
            jax.ShapeDtypeStruct(field.shape, jnp.bfloat16),
            jax.ShapeDtypeStruct((chans, rows, 4 * KZ), jnp.bfloat16),
        ],
        scratch_shapes=[
            pltpu.VMEM((chans, rows, 8 * KZ), jnp.bfloat16),
            pltpu.VMEM((chans * SUB, chans * SUB), jnp.bfloat16),
        ],
        compiler_params=pltpu.CompilerParams(vmem_limit_bytes=vmem_bytes),
    )(field, cot, spec, bias, skip, zt, back, yback)


def body(snapshots, cotangent, w_spec, first_moment, second_moment, w_skip, bias):
    chans, rows, length = snapshots.shape[1:]
    dp = lax.axis_size("dp")
    slab = lax.axis_size("slab")
    group = 64 * slab // KZ
    mode = np.arange(KY)
    ztop, zrest = halves(z_table())
    ones = np.zeros((2 * KZ, length), ml_dtypes.bfloat16)
    ones[:3] = 1
    back = jnp.asarray(np.concatenate([ztop.T, ztop.T, zrest.T, ones], 0))
    order = np.arange(2 * KZ).reshape(2, slab, -1).transpose(1, 0, 2).reshape(-1)
    zt = jnp.asarray(np.concatenate([ztop[:, order], zrest[:, order]], 1))
    ytop, yrest = halves(y_table(mode.reshape(-1, group).T.reshape(-1)))
    yt = np.concatenate([ytop, yrest], 1).reshape(slab, rows, -1)
    yt = jnp.asarray(np.ascontiguousarray(yt.transpose(0, 2, 1)))
    ytop, yrest = halves(y_table(mode.reshape(-1, 2).T.reshape(-1)))
    yback = jnp.asarray(np.concatenate([ytop, ytop, yrest], 1).reshape(slab, rows, -1))

    spec, u = forward_part(snapshots[0], zt, yt, w_spec, dp, slab)
    layer_out, zsum = point_part(
        snapshots[0], cotangent[0], spec, bias, w_skip, zt, back, yback
    )
    grad = grad_part(zsum, yt, u, dp, slab)
    new_first = 0.9 * first_moment + 0.1 * grad
    new_second = 0.95 * second_moment + 0.05 * grad * grad
    bias_first = 1.0 - 0.9**10
    bias_second = 1.0 - 0.95**10
    new_weights = w_spec - 0.01 * (new_first / bias_first) / (
        jnp.sqrt(new_second / bias_second) + 1e-08
    )
    return (layer_out[None], new_weights, new_first, new_second)


def solution(mesh):
    placed = (
        P("dp", None, "slab", None),
        P("dp", None, "slab", None),
        P("slab", "dp", None, None),
        P("slab", "dp", None, None),
        P("slab", "dp", None, None),
        P(),
        P(),
    )
    return jax.shard_map(
        body,
        mesh=mesh,
        in_specs=placed,
        out_specs=(
            P("dp", None, "slab", None),
            P("slab", "dp", None, None),
            P("slab", "dp", None, None),
            P("slab", "dp", None, None),
        ),
        check_vma=False,
    )
```

time: 142 us -> 122 us (0.86)
  Pallas kernels: 134 us -> 118 us
  local copies, waits for them, and re-layouts: 2.85 us -> 0.02 us
    pallas_call x1, Pallas kernels: 29.1 us -> 22.4 us  [grad_part(): pl.pallas_call(kernel, grid=(chans // per,), in_specs=[pl.BlockSpec((per,...]
    pallas_call x1, Pallas kernels: 50.3 us -> 44.4 us  [forward_part(): pl.pallas_call(kernel, grid=(chans // per,), in_specs=[pl.BlockSpec((per,...]
    pallas_call x1, Pallas kernels: 54.7 us -> 51.2 us  [point_part(): pl.pallas_call(point_kernel, grid=(rows // ROWS,), in_specs=[rowed, rowed...]
where the time goes in v2:
time: 122 us
  Pallas kernels  118 us (97%)
  other arithmetic  3.51 us (3%)
    pallas_call x1, Pallas kernels, point_part(): pl.pallas_call(point_kernel, grid=(rows // ROWS,), in_specs=[rowed, rowed...  51.2 us
    pallas_call x1, Pallas kernels, forward_part(): pl.pallas_call(kernel, grid=(chans // per,), in_specs=[pl.BlockSpec((per,...  44.4 us
    pallas_call x1, Pallas kernels, grad_part(): pl.pallas_call(kernel, grid=(chans // per,), in_specs=[pl.BlockSpec((per,...  22.4 us
    sub x1, other arithmetic, body(): w_spec - 0.01 * (new_first / bias_first) / (jnp.sqrt(new_second / bias_se...  3.51 us

profile of v2, /device:TPU:1, one launch (start us, length us, event | category | flops | bytes accessed | tf_op | source)
XLA Modules:
  0.0 122.2 jit_solution(1226165082927817754)
XLA Ops:
  0.6 44.4 %shard_map.138 = (f32[1024,128]{1,0:T(8,128)}, f32[512,128]{1,0:T(8,128)}) custom-call(bf16[64,256,512]{2,1,0:T(8,128)(2,1)} %bitcast.3, bf16[512,128]{1,0:T(8,128)(2,1)} %constant.27.clone.refs_1_.zt_ref, bf16[2,128,256]{2,1,0:T(8,128)(2,1)} %constant.28.clone.refs_2_.refs_1_, f32[16,2,64,128]{3,2,1,0:T(8,128)} %refs_3_.1), custom_call_target="tpu_custom_call" | custom-call | tf_op jit(solution)/shard_map/pallas_call | solution.py:474
  45.1 0.0 copy-start
  45.1 0.0 copy-start.1
  45.1 0.0 copy-start.2
  45.1 51.2 %shard_map.139 = (bf16[64,256,512]{2,1,0:T(8,128)(2,1)}, bf16[64,256,128]{2,1,0:T(8,128)(2,1)}) custom-call(bf16[64,256,512]{2,1,0:T(8,128)(2,1)} %bitcast.4, bf16[64,256,512]{2,1,0:T(8,128)(2,1)} %bitcast.5, f32[1024,128]{1,0:T(8,128)} %get-tuple-element.8.spec_ref, f32[64]{0:T(128)} %bias_ref.1, bf16[64,64]{1,0:T(8,128)(2,1)} %skip_ref.1, ...), custom_call_target="tpu_custom_call" | custom-call | tf_op jit(solution)/shard_map/pallas_call | solution.py:532
  96.3 22.4 %shard_map.140 = f32[16,2,64,128]{3,2,1,0:T(8,128)} custom-call(bf16[64,256,128]{2,1,0:T(8,128)(2,1)} %get-tuple-element.10.refs_0_, bf16[2,128,256]{2,1,0:T(8,128)(2,1)} %constant.28.clone.refs_2_.refs_1_, f32[512,128]{1,0:T(8,128)} %get-tuple-element.11.refs_2_), custom_call_target="tpu_custom_call" | custom-call | tf_op jit(solution)/shard_map/pallas_call | solution.py:510
  118.7 0.0 copy-done
  118.7 0.0 copy-done.1
  118.7 0.0 copy-done.2
  118.7 3.5 %divide_subtract_fusion = (f32[16,2,64,128]{3,2,1,0:T(8,128)}, f32[16,2,64,128]{3,2,1,0:T(8,128)}, f32[16,2,64,128]{3,2,1,0:T(8,128)}) fusion(f32[16,2,64,128]{3,2,1,0:T(8,128)S(1)} %copy-done, f32[16,2,64,128]{3,2,1,0:T(8,128)} %shard_map.140, f32[16,2,64,128]{3,2,1,0:T(8,128)S(1)} %copy-done.1, f32[16,2,64,128]{3,2,1,0:T(8,128)S(1)} %copy-done.2), kind=kLoop, calls=%fused_computation.2 | loop fusion | flops 3145728 | bytes 7340032 | tf_op jit(solution)/shard_map/sub | solution.py:577
Async XLA Ops:
  45.1 73.6 %copy-start = (f32[16,2,64,128]{3,2,1,0:T(8,128)S(1)}, f32[16,2,64,128]{3,2,1,0:T(8,128)}, u32[]{:S(2)}) copy-start(f32[16,2,64,128]{3,2,1,0:T(8,128)} %refs_3_.1) | copy-start | bytes 3145732
  45.1 73.6 %copy-start.1 = (f32[16,2,64,128]{3,2,1,0:T(8,128)S(1)}, f32[16,2,64,128]{3,2,1,0:T(8,128)}, u32[]{:S(2)}) copy-start(f32[16,2,64,128]{3,2,1,0:T(8,128)} %param.14) | copy-start | bytes 3145732
  45.1 73.6 %copy-start.2 = (f32[16,2,64,128]{3,2,1,0:T(8,128)S(1)}, f32[16,2,64,128]{3,2,1,0:T(8,128)}, u32[]{:S(2)}) copy-start(f32[16,2,64,128]{3,2,1,0:T(8,128)} %param.15) | copy-start | bytes 3145732

commit v3 on v2

--- a/solution.py
+++ b/solution.py
@@ -14,7 +14,7 @@
 KY = 32
 KZ = 32
 PAIRS = KY // 2
-ROWS = 16
+ROWS = 32
 SUB = 8
 
 gelu_coef = 0.7978845608028654
@@ -70,27 +70,29 @@
 
 
 def y_modes(both, ytab, slab):
+    wide = 4 * KZ
     both = mm(ytab, both)
     first = both[: 2 * KY]
-    w = first[:, : 2 * KZ] + first[:, 2 * KZ :] + both[2 * KY :, : 2 * KZ]
+    w = first[:, :wide] + first[:, wide:] + both[2 * KY :, :wide]
     per_k = KZ // slab
     group = 64 // per_k
     count = KY // group
-    lane = lax.broadcasted_iota(jnp.int32, (KY, 2 * KZ), 1)
+    lane = lax.broadcasted_iota(jnp.int32, (KY, wide), 1)
     real = lane % (2 * per_k) < per_k
     sine = w[KY:]
     ahead = jnp.concatenate([sine[:, per_k:], sine[:, :per_k]], axis=1)
-    behind = jnp.concatenate([sine[:, 2 * KZ - per_k :], sine[:, : 2 * KZ - per_k]], axis=1)
+    behind = jnp.concatenate([sine[:, wide - per_k :], sine[:, : wide - per_k]], axis=1)
     out = w[:KY] + jnp.where(real, ahead, -behind)
+
+    def piece(g, n):
+        return out[g * count : (g + 1) * count, n * 2 * per_k : (n + 1) * 2 * per_k]
+
     return [
-        jnp.concatenate(
-            [
-                out[g * count : (g + 1) * count, s * 2 * per_k : (s + 1) * 2 * per_k]
-                for g in range(group)
-            ],
-            axis=1,
-        )
-        for s in range(slab)
+        [
+            jnp.concatenate([piece(g, c * slab + s) for g in range(group)], axis=1)
+            for s in range(slab)
+        ]
+        for c in range(2)
     ]
 
 
@@ -133,11 +135,13 @@
         )
 
     def chunk(self, step, per, halves_of, ytab, part, near, sems):
-        rows = per * self.count
+        rows = per * 2 * self.count
         start = pl.multiple_of(step * rows, rows)
-        for c in range(per):
-            for s, value in enumerate(y_modes(halves_of(c), ytab, self.slab)):
-                part[s, pl.ds(start + c * self.count, self.count), :] = value
+        for n in range(per):
+            for c, shares in enumerate(y_modes(halves_of(n), ytab, self.slab)):
+                for s, value in enumerate(shares):
+                    place = start + (2 * n + c) * self.count
+                    part[s, pl.ds(place, self.count), :] = value
 
         @pl.when(step == 0)
         def _():
@@ -288,20 +292,21 @@
 ):
     links = Links(dp, slab)
     step = pl.program_id(0)
-    per, rows, length = x_ref.shape
+    per, _, rows, length = x_ref.shape
     chans = part.shape[1] // links.count
     area = links.area
-    steps = chans // per
+    steps = chans // per // 2
 
     @pl.when(step == 0)
     def _():
         links.greet()
 
-    zval = mm(x_ref[...].reshape(per * rows, length), zt_ref[...])
-    zval = (zval[:, : 2 * KZ] + zval[:, 2 * KZ :]).reshape(per, rows, 2 * KZ)
-
-    def halves_of(c):
-        return jnp.concatenate(split(zval[c]), axis=1)
+    sides = [x_ref[:, c].reshape(per * rows, length) for c in range(2)]
+    zval = mm(jnp.concatenate(sides, axis=1), zt_ref[: 2 * length])
+    zval = (zval[:, : 4 * KZ] + zval[:, 4 * KZ :]).reshape(per, rows, 4 * KZ)
+
+    def halves_of(n):
+        return jnp.concatenate(split(zval[n]), axis=1)
 
     links.chunk(step, per, halves_of, yt_ref[links.me_s], part, near, sems[:4])
 
@@ -340,13 +345,13 @@
     per = z_ref.shape[0]
     chans = part.shape[1] // links.count
     area = links.area
-    steps = chans // per
+    steps = chans // per // 2
 
     @pl.when(step == 0)
     def _():
         links.greet()
 
-    links.chunk(step, per, lambda c: z_ref[c], yt_ref[links.me_s], part, near, sems)
+    links.chunk(step, per, lambda n: z_ref[n], yt_ref[links.me_s], part, near, sems)
 
     @pl.when(step == pl.num_programs(0) - 1)
     def _():
@@ -372,20 +377,27 @@
 
 def point_kernel(
     x_ref, cot_ref, spec_ref, bias_ref, skip_ref, zt_ref, back_ref, yback_ref,
-    out_ref, z_ref, left, kron_ref,
+    out_ref, z_ref, left, kron_ref, xs, tops, rests,
 ):
     step = pl.program_id(0)
-    chans, rows = left.shape[:2]
+    groups, tall = left.shape[:2]
+    chans = tall // SUB
+    half = tall // 2
+    rows = groups * SUB
     wide = 2 * KZ
     me_s = lax.axis_index("slab")
 
     @pl.when(step == 0)
     def _():
-        tall = chans * SUB
         part = tall // 4
         spread = one_hot((chans, tall), lambda i, r: i == r // SUB)
         for m in range(4):
-            pick = one_hot((part, chans), lambda r, o: (r + m * part) // SUB == o)
+
+            def channel(r):
+                r = r + m * part
+                return r % half // SUB * 2 + r // half
+
+            pick = one_hot((part, chans), lambda r, o: channel(r) == o)
             rows_of = lax.dot_general(
                 pick, skip_ref[...], (((1,), (1,)), ((), ())), preferred_element_type=jnp.float32
             ).astype(jnp.bfloat16)
@@ -395,45 +407,97 @@
             )
         yback = yback_ref[me_s]
 
-        def invert(o):
-            pairs = spec_ref[pl.ds(pl.multiple_of(o * PAIRS, PAIRS), PAIRS), :]
-            v = jnp.concatenate([pairs[:, :wide], pairs[:, wide:]], axis=0)
-            turned = jnp.concatenate([-v[:, KZ:], v[:, :KZ]], axis=1)
+        def three(o):
+            b = jnp.full((rows, 2 * wide), bias_ref[o], jnp.float32)
+            b0 = b.astype(jnp.bfloat16).astype(jnp.float32)
+            b1 = (b - b0).astype(jnp.bfloat16).astype(jnp.float32)
+            lane = lax.broadcasted_iota(jnp.int32, b.shape, 1) - wide
+            return jnp.where(lane == 0, b0, jnp.where(lane == 1, b1, b - b0 - b1))
+
+        def invert(n):
+            two = [
+                spec_ref[pl.ds(pl.multiple_of((2 * n + c) * PAIRS, PAIRS), PAIRS), :]
+                for c in range(2)
+            ]
+            v = jnp.concatenate(
+                [
+                    jnp.concatenate([two[0][:, :wide], two[1][:, :wide]], axis=1),
+                    jnp.concatenate([two[0][:, wide:], two[1][:, wide:]], axis=1),
+                ],
+                axis=0,
+            )
+            turned = jnp.concatenate(
+                [-v[:, KZ:wide], v[:, :KZ], -v[:, wide + KZ :], v[:, wide : wide + KZ]], axis=1
+            )
             top, rest = split(jnp.concatenate([v, turned], axis=0))
             yval = mm(yback, jnp.concatenate([top, rest, top], axis=0))
-            ytop, yrest = split(yval)
-            b = jnp.full((1, wide), bias_ref[o], jnp.float32)
-            b0 = b.astype(jnp.bfloat16).astype(jnp.float32)
-            b1 = (b - b0).astype(jnp.bfloat16).astype(jnp.float32)
-            lane = lax.broadcasted_iota(jnp.int32, b.shape, 1)
-            terms = jnp.where(lane == 0, b0, jnp.where(lane == 1, b1, b - b0 - b1))
-            terms = jnp.broadcast_to(terms, (rows, wide)).astype(jnp.bfloat16)
-            left[o] = jnp.concatenate([ytop, yrest, ytop, terms], axis=1)
-
-        each(chans, invert)
-
-    here = pl.ds(pl.multiple_of(step * ROWS, ROWS), ROWS)
+            high = yval.astype(jnp.bfloat16).astype(jnp.float32)
+            low = yval - high
+            high_turned, low_turned = halves_swapped(high), halves_swapped(low)
+            first = lax.broadcasted_iota(jnp.int32, high.shape, 1) < wide
+            even = [
+                jnp.where(first, high, low_turned),
+                jnp.where(first, high, three(2 * n)),
+            ]
+            odd = [
+                jnp.where(first, high_turned, low),
+                jnp.where(first, high_turned, three(2 * n + 1)),
+            ]
+            return [
+                jnp.concatenate(side, axis=1).reshape(groups, SUB, 4 * wide)
+                for side in (even, odd)
+            ]
+
+        def invert_two(n):
+            one, two = invert(2 * n), invert(2 * n + 1)
+            for c in range(2):
+                place = pl.multiple_of(c * half + n * 2 * SUB, 2 * SUB)
+                left[:, pl.ds(place, 2 * SUB), :] = jnp.concatenate(
+                    [one[c], two[c]], axis=1
+                ).astype(jnp.bfloat16)
+
+        each(chans // 4, invert_two)
+
+    per = x_ref.shape[1] // SUB
     field = x_ref[...].astype(jnp.float32)
-    terms = left[:, here, :].astype(jnp.float32)
-    values, sums = [], []
-    for m in range(ROWS // SUB):
+    for m in range(per):
         own = slice(m * SUB, (m + 1) * SUB)
-        x = field[:, own].reshape(chans * SUB, NZ).astype(jnp.bfloat16)
-        term = terms[:, own].reshape(chans * SUB, 4 * wide).astype(jnp.bfloat16)
-        pre = mm(kron_ref[...], x) + mm(term, back_ref[...])
+        xs[m] = field[:, own].reshape(tall, NZ).astype(jnp.bfloat16)
+
+    values = [[None] * per for _ in range(2)]
+
+    def piece(c, m):
+        these = slice(c * half, (c + 1) * half)
+        own = slice(m * SUB, (m + 1) * SUB)
+        pre = mm(kron_ref[these, :], xs[m]) + mm(left[step * per + m, these, :], back_ref[...])
         sq = pre * pre
-        t = jnp.tanh(pre * (gelu_coef + (gelu_coef * cube_coef) * sq))
+        p = (gelu_coef * cube_coef) * sq
+        t = jnp.tanh(pre * (gelu_coef + p))
         h = 0.5 + 0.5 * t
         value = pre * h
-        values.append(value.reshape(chans, SUB, NZ))
-        grow = 2.0 * gelu_coef + (6.0 * gelu_coef * cube_coef) * sq
-        cot = cot_ref[...].astype(jnp.float32)[:, own].reshape(chans * SUB, NZ)
-        slope = cot * (h + value * (0.5 - 0.5 * t) * grow)
+        values[c][m] = value.reshape(chans // 2, SUB, NZ)
+        grow = 2.0 * gelu_coef + 6.0 * p
+        cot = cot_ref[:, c].astype(jnp.float32)[:, own].reshape(half, NZ)
+        slope = cot * (h + (value - value * h) * grow)
         top, rest = split(slope)
-        zval = mm(top, zt_ref[...])
-        zval = zval[:, :wide] + zval[:, wide:] + mm(rest, zt_ref[:, :wide])
-        sums.append(zval.reshape(chans, SUB, wide))
-    out_ref[...] = jnp.concatenate(values, axis=1).astype(jnp.bfloat16)
+        tops[m, these, :] = top
+        rests[m, these, :] = rest
+        if m % 2 == 1:
+            both = jnp.concatenate(values[c][m - 1 : m + 1], axis=1).astype(jnp.bfloat16)
+            out_ref[:, c, (m - 1) * SUB : (m + 1) * SUB, :] = both
+
+    for m in range(per):
+        for c in range(2):
+            piece(c, m)
+
+    sides = [
+        jnp.concatenate([held[m, c * half : (c + 1) * half, :] for m in range(per)], axis=0)
+        for held in (tops, rests)
+        for c in range(2)
+    ]
+    zval = mm(jnp.concatenate(sides, axis=1), zt_ref[...])
+    zval = zval[:, : 2 * wide] + zval[:, 2 * wide :]
+    sums = [zval[m * half : (m + 1) * half].reshape(chans // 2, SUB, 2 * wide) for m in range(per)]
     z_ref[...] = jnp.concatenate(split(jnp.concatenate(sums, axis=1)), axis=2)
 
 
@@ -466,6 +530,7 @@
     chans, rows, length = field.shape
     per = 8
     area = (KY // dp) * (KZ // slab)
+    field = field.reshape(chans // 2, 2, rows, length)
     wide = 2 * chans
 
     def kernel(*refs):
@@ -473,9 +538,9 @@
 
     return pl.pallas_call(
         kernel,
-        grid=(chans // per,),
+        grid=(chans // 2 // per,),
         in_specs=[
-            pl.BlockSpec((per, rows, length), lambda i: (i, 0, 0)),
+            pl.BlockSpec((per, 2, rows, length), lambda i: (i, 0, 0, 0)),
             whole(zt.shape),
             whole(yt.shape),
             whole(w_spec.shape),
@@ -491,7 +556,7 @@
             pltpu.VMEM((dp * area, wide), jnp.float32),
             pltpu.VMEM((slab, dp, area, wide), jnp.float32),
         ]
-        + link_sems(dp, slab, chans // per)
+        + link_sems(dp, slab, chans // 2 // per)
         + link_sems(dp, slab, dp),
         compiler_params=pltpu.CompilerParams(
             vmem_limit_bytes=vmem_bytes, collective_id=0, has_side_effects=True
@@ -500,7 +565,8 @@
 
 
 def grad_part(zsum, yt, u, dp, slab):
-    chans, rows, width = zsum.shape
+    pairs, rows, width = zsum.shape
+    chans = 2 * pairs
     per = 8
     per_j, per_k = KY // dp, KZ // slab
 
@@ -509,7 +575,7 @@
 
     return pl.pallas_call(
         kernel,
-        grid=(chans // per,),
+        grid=(pairs // per,),
         in_specs=[
             pl.BlockSpec((per, rows, width), lambda i: (i, 0, 0)),
             whole(yt.shape),
@@ -519,7 +585,7 @@
         out_shape=jax.ShapeDtypeStruct((per_k, per_j, chans, 2 * chans), jnp.float32),
         scratch_shapes=link_scratch(dp, slab, chans)
         + [pltpu.VMEM((per_j * per_k, chans, 6 * dp), jnp.bfloat16)]
-        + link_sems(dp, slab, chans // per),
+        + link_sems(dp, slab, chans // 2 // per),
         compiler_params=pltpu.CompilerParams(
             vmem_limit_bytes=vmem_bytes, collective_id=1, has_side_effects=True
         ),
@@ -528,23 +594,34 @@
 
 def point_part(field, cot, spec, bias, skip, zt, back, yback):
     chans, rows, length = field.shape
-    rowed = pl.BlockSpec((chans, ROWS, length), lambda i: (0, i, 0))
-    return pl.pallas_call(
+    paired = (chans // 2, 2, rows, length)
+    two = pl.BlockSpec((chans // 2, 2, ROWS, length), lambda i: (0, 0, i, 0))
+    held = pltpu.VMEM((ROWS // SUB, chans * SUB, length), jnp.bfloat16)
+    out, zsum = pl.pallas_call(
         point_kernel,
         grid=(rows // ROWS,),
-        in_specs=[rowed, rowed, whole(spec.shape), pl.BlockSpec(memory_space=pltpu.SMEM)]
+        in_specs=[
+            pl.BlockSpec((chans, ROWS, length), lambda i: (0, i, 0)),
+            two,
+            whole(spec.shape),
+            pl.BlockSpec(memory_space=pltpu.SMEM),
+        ]
         + [whole(a.shape) for a in (skip, zt, back, yback)],
-        out_specs=[rowed, pl.BlockSpec((chans, ROWS, 4 * KZ), lambda i: (0, i, 0))],
+        out_specs=[two, pl.BlockSpec((chans // 2, ROWS, 8 * KZ), lambda i: (0, i, 0))],
         out_shape=[
-            jax.ShapeDtypeStruct(field.shape, jnp.bfloat16),
-            jax.ShapeDtypeStruct((chans, rows, 4 * KZ), jnp.bfloat16),
+            jax.ShapeDtypeStruct(paired, jnp.bfloat16),
+            jax.ShapeDtypeStruct((chans // 2, rows, 8 * KZ), jnp.bfloat16),
         ],
         scratch_shapes=[
-            pltpu.VMEM((chans, rows, 8 * KZ), jnp.bfloat16),
+            pltpu.VMEM((rows // SUB, chans * SUB, 8 * KZ), jnp.bfloat16),
             pltpu.VMEM((chans * SUB, chans * SUB), jnp.bfloat16),
+            held,
+            held,
+            held,
         ],
         compiler_params=pltpu.CompilerParams(vmem_limit_bytes=vmem_bytes),
-    )(field, cot, spec, bias, skip, zt, back, yback)
+    )(field, cot.reshape(paired), spec, bias, skip, zt, back, yback)
+    return out.reshape(field.shape), zsum
 
 
 def body(snapshots, cotangent, w_spec, first_moment, second_moment, w_skip, bias):
@@ -558,7 +635,15 @@
     ones[:3] = 1
     back = jnp.asarray(np.concatenate([ztop.T, ztop.T, zrest.T, ones], 0))
     order = np.arange(2 * KZ).reshape(2, slab, -1).transpose(1, 0, 2).reshape(-1)
-    zt = jnp.asarray(np.concatenate([ztop[:, order], zrest[:, order]], 1))
+    ztop, zrest = ztop[:, order], zrest[:, order]
+    none = np.zeros_like(ztop)
+    zt = [
+        [ztop, none, zrest, none],
+        [none, ztop, none, zrest],
+        [ztop, none, none, none],
+        [none, ztop, none, none],
+    ]
+    zt = jnp.asarray(np.block(zt))
     ytop, yrest = halves(y_table(mode.reshape(-1, group).T.reshape(-1)))
     yt = np.concatenate([ytop, yrest], 1).reshape(slab, rows, -1)
     yt = jnp.asarray(np.ascontiguousarray(yt.transpose(0, 2, 1)))

time: 122 us -> 103 us (0.84)
  Pallas kernels: 118 us -> 99 us
    pallas_call x3, Pallas kernels: 118 us -> 99 us  [the longest x1 39.1 us: forward_part(): pl.pallas_call(kernel, grid=(chans // 2 // per,), in_specs=[pl.BlockSpec(...]
where the time goes in v3:
time: 103 us
  Pallas kernels  99 us (96%)
  other arithmetic  3.51 us (3%)
    pallas_call x1, Pallas kernels, forward_part(): pl.pallas_call(kernel, grid=(chans // 2 // per,), in_specs=[pl.BlockSpec(...  39.1 us
    pallas_call x1, Pallas kernels, point_part(): pl.pallas_call(point_kernel, grid=(rows // ROWS,), in_specs=[pl.BlockSpec...  38.5 us
    pallas_call x1, Pallas kernels, grad_part(): pl.pallas_call(kernel, grid=(pairs // per,), in_specs=[pl.BlockSpec((per,...  21.3 us
    sub x1, other arithmetic, body(): w_spec - 0.01 * (new_first / bias_first) / (jnp.sqrt(new_second / bias_se...  3.51 us

profile of v3, /device:TPU:1, one launch (start us, length us, event | category | flops | bytes accessed | tf_op | source)
XLA Modules:
  0.0 103.2 jit_solution(14466851275111052964)
XLA Ops:
  0.6 39.1 %shard_map.138 = (f32[1024,128]{1,0:T(8,128)}, f32[512,128]{1,0:T(8,128)}) custom-call(bf16[32,2,256,512]{3,2,1,0:T(8,128)(2,1)} %bitcast.4, bf16[2048,256]{1,0:T(8,128)(2,1)} %constant.27.clone.refs_1_.zt_ref, bf16[2,128,256]{2,1,0:T(8,128)(2,1)} %constant.28.clone.refs_2_.refs_1_, f32[16,2,64,128]{3,2,1,0:T(8,128)} %refs_3_.1), custom_call_target="tpu_custom_call" | custom-call | tf_op jit(solution)/shard_map/pallas_call | solution.py:539
  39.8 0.0 copy-start
  39.8 0.0 copy-start.1
  39.8 0.0 copy-start.2
  39.8 38.5 %shard_map.139 = (bf16[32,2,256,512]{3,2,1,0:T(8,128)(2,1)}, bf16[32,256,256]{2,1,0:T(8,128)(2,1)}) custom-call(bf16[64,256,512]{2,1,0:T(8,128)(2,1)} %bitcast.5, bf16[32,2,256,512]{3,2,1,0:T(8,128)(2,1)} %bitcast.6, f32[1024,128]{1,0:T(8,128)} %get-tuple-element.8.spec_ref, f32[64]{0:T(128)} %bias_ref.1, bf16[64,64]{1,0:T(8,128)(2,1)} %skip_ref.1, ...), custom_call_target="tpu_custom_call" | custom-call | tf_op jit(solution)/shard_map/pallas_call | solution.py:600
  78.3 21.3 %shard_map.140 = f32[16,2,64,128]{3,2,1,0:T(8,128)} custom-call(bf16[32,256,256]{2,1,0:T(8,128)(2,1)} %get-tuple-element.10.refs_0_, bf16[2,128,256]{2,1,0:T(8,128)(2,1)} %constant.28.clone.refs_2_.refs_1_, f32[512,128]{1,0:T(8,128)} %get-tuple-element.11.refs_2_), custom_call_target="tpu_custom_call" | custom-call | tf_op jit(solution)/shard_map/pallas_call | solution.py:576
  99.7 0.0 copy-done
  99.7 0.0 copy-done.1
  99.7 0.0 copy-done.2
  99.7 3.5 %divide_subtract_fusion = (f32[16,2,64,128]{3,2,1,0:T(8,128)}, f32[16,2,64,128]{3,2,1,0:T(8,128)}, f32[16,2,64,128]{3,2,1,0:T(8,128)}) fusion(f32[16,2,64,128]{3,2,1,0:T(8,128)S(1)} %copy-done, f32[16,2,64,128]{3,2,1,0:T(8,128)} %shard_map.140, f32[16,2,64,128]{3,2,1,0:T(8,128)S(1)} %copy-done.1, f32[16,2,64,128]{3,2,1,0:T(8,128)S(1)} %copy-done.2), kind=kLoop, calls=%fused_computation.2 | loop fusion | flops 3145728 | bytes 7340032 | tf_op jit(solution)/shard_map/sub | solution.py:662
Async XLA Ops:
  39.8 59.9 %copy-start = (f32[16,2,64,128]{3,2,1,0:T(8,128)S(1)}, f32[16,2,64,128]{3,2,1,0:T(8,128)}, u32[]{:S(2)}) copy-start(f32[16,2,64,128]{3,2,1,0:T(8,128)} %refs_3_.1) | copy-start | bytes 3145732
  39.8 59.9 %copy-start.1 = (f32[16,2,64,128]{3,2,1,0:T(8,128)S(1)}, f32[16,2,64,128]{3,2,1,0:T(8,128)}, u32[]{:S(2)}) copy-start(f32[16,2,64,128]{3,2,1,0:T(8,128)} %param.14) | copy-start | bytes 3145732
  39.8 59.9 %copy-start.2 = (f32[16,2,64,128]{3,2,1,0:T(8,128)S(1)}, f32[16,2,64,128]{3,2,1,0:T(8,128)}, u32[]{:S(2)}) copy-start(f32[16,2,64,128]{3,2,1,0:T(8,128)} %param.15) | copy-start | bytes 3145732

commit v4 on v3

--- a/solution.py
+++ b/solution.py
@@ -152,55 +152,62 @@
 
     def to_owner(self, steps, part, near, total, got, sems):
         far_send, far_recv = sems[2:]
-        dp, slab, me_d, me_s, area = self.dp, self.slab, self.me_d, self.me_s, self.area
+        dp, slab, me_d, me_s = self.dp, self.slab, self.me_d, self.me_s
+        area, some = self.area // 2, self.per_k // 2
         rows = part.shape[1] // steps
-        chans = part.shape[1] // self.count
-
-        @pl.loop(0, steps)
-        def _(step):
-            for t in range(1, slab):
-                self.near_copy(step, rows, part, near, sems, t).wait_recv()
-
-        def far_copy(d):
-            return self.copy(
-                total.at[d], got.at[pl.ds(me_d * area, area)],
-                far_send.at[d], far_recv.at[me_d], d, me_s,
-            )
-
+        chans = part.shape[1] // self.count // 2
         owners = self.group // self.per_j
         first = lax.div(lax.rem(me_d + 1, dp), owners)
 
-        @pl.loop(0, self.count)
-        def _(n):
-            q = lax.rem(first + n, self.count)
-            own = pl.ds(q, chans, stride=self.count)
-            value = part[me_s, own, :]
-            for t in range(1, slab):
-                value = value + near[t - 1, own, :]
-            turned = value.T
-            for g in range(self.group):
-                block = turned[2 * g * self.per_k : 2 * (g + 1) * self.per_k]
-                place = (g % self.per_j) * self.per_k
-                d = q * owners + g // self.per_j
-                total[d, place : place + self.per_k, :] = jnp.concatenate(
-                    [block[: self.per_k], block[self.per_k :]], axis=1
-                )
-            for g in range(owners):
-                d = q * owners + g
-
-                @pl.when(d != me_d)
-                def _():
-                    far_copy(d).start()
-
-        got[pl.ds(me_d * area, area), :] = total[me_d]
-
-        @pl.loop(0, dp - 1)
-        def _(n):
-            src = lax.rem(me_d + dp - 1 - n, dp)
-            self.copy(
-                total.at[src], got.at[pl.ds(src * area, area)],
-                far_send.at[src], far_recv.at[src], src, me_s,
-            ).wait_recv()
+        def place_of(h, d):
+            return pl.ds((h * dp + d) * area, area)
+
+        def far_copy(h, d):
+            return self.copy(
+                total.at[h, d], got.at[place_of(h, me_d)],
+                far_send.at[h, d], far_recv.at[h, me_d], d, me_s,
+            )
+
+        for h in range(2):
+
+            @pl.loop(h * steps // 2, (h + 1) * steps // 2)
+            def _(step):
+                for t in range(1, slab):
+                    self.near_copy(step, rows, part, near, sems, t).wait_recv()
+
+            @pl.loop(0, self.count)
+            def _(n):
+                q = lax.rem(first + n, self.count)
+                own = pl.ds(h * chans * self.count + q, chans, stride=self.count)
+                value = part[me_s, own, :]
+                for t in range(1, slab):
+                    value = value + near[t - 1, own, :]
+                turned = value.T
+                for g in range(self.group):
+                    block = turned[2 * g * self.per_k : 2 * (g + 1) * self.per_k]
+                    place = (g % self.per_j) * some
+                    d = q * owners + g // self.per_j
+                    total[h, d, place : place + some, :] = jnp.concatenate(
+                        [block[n * some : (n + 1) * some] for n in (0, 2, 1, 3)], axis=1
+                    )
+                for g in range(owners):
+                    d = q * owners + g
+
+                    @pl.when(d != me_d)
+                    def _():
+                        far_copy(h, d).start()
+
+            got[place_of(h, me_d), :] = total[h, me_d]
+
+        for h in range(2):
+
+            @pl.loop(0, dp - 1)
+            def _(n):
+                src = lax.rem(me_d + dp - 1 - n, dp)
+                self.copy(
+                    total.at[h, src], got.at[place_of(h, src)],
+                    far_send.at[h, src], far_recv.at[h, src], src, me_s,
+                ).wait_recv()
 
         @pl.loop(0, steps)
         def _(step):
@@ -209,7 +216,20 @@
 
         @pl.loop(0, dp - 1)
         def _(n):
-            far_copy(lax.rem(me_d + 1 + n, dp)).wait_send()
+            d = lax.rem(me_d + 1 + n, dp)
+            for h in range(2):
+                far_copy(h, d).wait_send()
+
+    def owned(self, got, r):
+        area, some = self.area // 2, self.per_k // 2
+        one = got[pl.ds(r, self.dp, stride=area), :]
+        two = got[pl.ds(self.dp * area + r, self.dp, stride=area), :]
+        low = lax.broadcasted_iota(jnp.int32, one.shape, 1) < one.shape[1] // 2
+        row = lax.div(r, some) * self.per_k + lax.rem(r, some)
+        return [
+            (row, jnp.where(low, one, halves_swapped(two))),
+            (row + some, jnp.where(low, halves_swapped(one), two)),
+        ]
 
     def from_owner(self, values, back, spec, sems):
         near_send, near_recv, far_send, far_recv = sems
@@ -316,7 +336,9 @@
             w = w_ref[lax.rem(r, links.per_k), lax.div(r, links.per_k)]
             low = lax.broadcasted_iota(jnp.int32, w.shape, 1) < chans
             turned = halves_swapped(w)
-            both = jnp.concatenate([w, jnp.where(low, -turned, turned)], axis=0)
+            turned = jnp.where(low, -turned, turned)
+            few = chans // 2
+            both = jnp.concatenate([w[:few], turned[:few], w[few:], turned[few:]], axis=0)
             top, rest = split(both)
             mixer[r] = jnp.concatenate([top, rest], axis=1)
 
@@ -324,15 +346,15 @@
         links.to_owner(steps, part, near, total, got, sems[:4])
         scale = 1.0 / math.sqrt(NY * NZ) / math.sqrt(KY * KZ)
 
-        def mix(r):
-            u = got[pl.ds(r, dp, stride=area), :]
-            top, rest = split(u)
-            out = mm(jnp.concatenate([top, rest], axis=0), mixer[r])
-            wide = 2 * chans
-            v = out[:dp, :wide] + out[:dp, wide:] + out[dp:, :wide]
-            values[pl.ds(r, dp, stride=area), :] = v * scale
-
-        each(area, mix)
+        def mix(pair):
+            for r, u in links.owned(got, pair):
+                top, rest = split(u)
+                out = mm(jnp.concatenate([top, rest], axis=0), mixer[r])
+                wide = 2 * chans
+                v = out[:dp, :wide] + out[:dp, wide:] + out[dp:, :wide]
+                values[pl.ds(r, dp, stride=area), :] = v * scale
+
+        each(area // 2, mix)
         u_ref[...] = got[...]
         links.from_owner(values, back, spec_ref, sems[4:])
 
@@ -355,24 +377,32 @@
 
     @pl.when(step == pl.num_programs(0) - 1)
     def _():
-        def prepare(r):
-            turned = u_ref[pl.ds(r, dp, stride=area), :].T
-            top, rest = split(jnp.concatenate([turned[:chans], turned[chans:]], axis=1))
-            left[r] = jnp.concatenate([top, top, rest], axis=1)
-
-        each(area, prepare)
+        few = chans // 2
+
+        def prepare(pair):
+            for r, u in links.owned(u_ref, pair):
+                turned = u.T
+                real = jnp.concatenate([turned[:few], turned[2 * few : 3 * few]], axis=0)
+                imag = jnp.concatenate([turned[few : 2 * few], turned[3 * few :]], axis=0)
+                top, rest = split(jnp.concatenate([real, imag], axis=1))
+                left[r] = jnp.concatenate([top, top, rest], axis=1)
+
+        each(area // 2, prepare)
         links.to_owner(steps, part, near, total, got, sems)
         scale = 1.0 / math.sqrt(NY * NZ) / math.sqrt(KY * KZ) / dp
 
-        def multiply(r):
-            g = got[pl.ds(r, dp, stride=area), :]
-            low = lax.broadcasted_iota(jnp.int32, g.shape, 1) < chans
-            turned = halves_swapped(g)
-            top, rest = split(jnp.concatenate([g, jnp.where(low, turned, -turned)], axis=0))
-            grad = mm(left[r], jnp.concatenate([top, rest, top], axis=0))
-            grad_ref[lax.rem(r, links.per_k), lax.div(r, links.per_k)] = grad * scale
-
-        each(area, multiply)
+        def multiply(pair):
+            for r, g in links.owned(got, pair):
+                g = jnp.concatenate(
+                    [g[:, n * few : (n + 1) * few] for n in (0, 2, 1, 3)], axis=1
+                )
+                low = lax.broadcasted_iota(jnp.int32, g.shape, 1) < chans
+                turned = halves_swapped(g)
+                top, rest = split(jnp.concatenate([g, jnp.where(low, turned, -turned)], axis=0))
+                grad = mm(left[r], jnp.concatenate([top, rest, top], axis=0))
+                grad_ref[lax.rem(r, links.per_k), lax.div(r, links.per_k)] = grad * scale
+
+        each(area // 2, multiply)
 
 
 def point_kernel(
@@ -512,17 +542,17 @@
     return [
         pltpu.VMEM((slab, rows, 128), jnp.float32),
         pltpu.VMEM((slab - 1, rows, 128), jnp.float32),
-        pltpu.VMEM((dp, area, wide), jnp.float32),
+        pltpu.VMEM((2, dp, area // 2, wide), jnp.float32),
         pltpu.VMEM((dp * area, wide), jnp.float32),
     ]
 
 
-def link_sems(dp, slab, steps):
+def link_sems(slab, steps, far):
     return [
         pltpu.SemaphoreType.DMA((slab - 1, steps)),
         pltpu.SemaphoreType.DMA((slab - 1, steps)),
-        pltpu.SemaphoreType.DMA((dp,)),
-        pltpu.SemaphoreType.DMA((dp,)),
+        pltpu.SemaphoreType.DMA(far),
+        pltpu.SemaphoreType.DMA(far),
     ]
 
 
@@ -556,8 +586,8 @@
             pltpu.VMEM((dp * area, wide), jnp.float32),
             pltpu.VMEM((slab, dp, area, wide), jnp.float32),
         ]
-        + link_sems(dp, slab, chans // 2 // per)
-        + link_sems(dp, slab, dp),
+        + link_sems(slab, chans // 2 // per, (2, dp))
+        + link_sems(slab, dp, (dp,)),
         compiler_params=pltpu.CompilerParams(
             vmem_limit_bytes=vmem_bytes, collective_id=0, has_side_effects=True
         ),
@@ -585,7 +615,7 @@
         out_shape=jax.ShapeDtypeStruct((per_k, per_j, chans, 2 * chans), jnp.float32),
         scratch_shapes=link_scratch(dp, slab, chans)
         + [pltpu.VMEM((per_j * per_k, chans, 6 * dp), jnp.bfloat16)]
-        + link_sems(dp, slab, chans // 2 // per),
+        + link_sems(slab, chans // 2 // per, (2, dp)),
         compiler_params=pltpu.CompilerParams(
             vmem_limit_bytes=vmem_bytes, collective_id=1, has_side_effects=True
         ),

time: 103 us -> 103 us (level)
    pallas_call x1, Pallas kernels: 39.1 us -> 37.6 us  [forward_part(): pl.pallas_call(kernel, grid=(chans // 2 // per,), in_specs=[pl.BlockSpec(...]
    pallas_call x1, Pallas kernels: 21.3 us -> 22.5 us  [grad_part(): pl.pallas_call(kernel, grid=(pairs // per,), in_specs=[pl.BlockSpec((per,...]
where the time goes in v4:
time: 103 us
  Pallas kernels  98.6 us (96%)
  other arithmetic  3.51 us (3%)
    pallas_call x1, Pallas kernels, point_part(): pl.pallas_call(point_kernel, grid=(rows // ROWS,), in_specs=[pl.BlockSpec...  38.5 us
    pallas_call x1, Pallas kernels, forward_part(): pl.pallas_call(kernel, grid=(chans // 2 // per,), in_specs=[pl.BlockSpec(...  37.6 us
    pallas_call x1, Pallas kernels, grad_part(): pl.pallas_call(kernel, grid=(pairs // per,), in_specs=[pl.BlockSpec((per,...  22.5 us
    sub x1, other arithmetic, body(): w_spec - 0.01 * (new_first / bias_first) / (jnp.sqrt(new_second / bias_se...  3.51 us

profile of v4, /device:TPU:1, one launch (start us, length us, event | category | flops | bytes accessed | tf_op | source)
XLA Modules:
  0.0 102.8 jit_solution(11939738113388838712)
XLA Ops:
  0.6 37.6 %shard_map.138 = (f32[1024,128]{1,0:T(8,128)}, f32[512,128]{1,0:T(8,128)}) custom-call(bf16[32,2,256,512]{3,2,1,0:T(8,128)(2,1)} %bitcast.4, bf16[2048,256]{1,0:T(8,128)(2,1)} %constant.27.clone.refs_1_.zt_ref, bf16[2,128,256]{2,1,0:T(8,128)(2,1)} %constant.28.clone.refs_2_.refs_1_, f32[16,2,64,128]{3,2,1,0:T(8,128)} %refs_3_.1), custom_call_target="tpu_custom_call" | custom-call | tf_op jit(solution)/shard_map/pallas_call | solution.py:569
  38.2 0.0 copy-start
  38.2 0.0 copy-start.1
  38.2 0.0 copy-start.2
  38.3 38.5 %shard_map.139 = (bf16[32,2,256,512]{3,2,1,0:T(8,128)(2,1)}, bf16[32,256,256]{2,1,0:T(8,128)(2,1)}) custom-call(bf16[64,256,512]{2,1,0:T(8,128)(2,1)} %bitcast.5, bf16[32,2,256,512]{3,2,1,0:T(8,128)(2,1)} %bitcast.6, f32[1024,128]{1,0:T(8,128)} %get-tuple-element.8.spec_ref, f32[64]{0:T(128)} %bias_ref.1, bf16[64,64]{1,0:T(8,128)(2,1)} %skip_ref.1, ...), custom_call_target="tpu_custom_call" | custom-call | tf_op jit(solution)/shard_map/pallas_call | solution.py:630
  76.8 22.5 %shard_map.140 = f32[16,2,64,128]{3,2,1,0:T(8,128)} custom-call(bf16[32,256,256]{2,1,0:T(8,128)(2,1)} %get-tuple-element.10.refs_0_, bf16[2,128,256]{2,1,0:T(8,128)(2,1)} %constant.28.clone.refs_2_.refs_1_, f32[512,128]{1,0:T(8,128)} %get-tuple-element.11.refs_2_), custom_call_target="tpu_custom_call" | custom-call | tf_op jit(solution)/shard_map/pallas_call | solution.py:606
  99.3 0.0 copy-done
  99.3 0.0 copy-done.1
  99.3 0.0 copy-done.2
  99.3 3.5 %divide_subtract_fusion = (f32[16,2,64,128]{3,2,1,0:T(8,128)}, f32[16,2,64,128]{3,2,1,0:T(8,128)}, f32[16,2,64,128]{3,2,1,0:T(8,128)}) fusion(f32[16,2,64,128]{3,2,1,0:T(8,128)S(1)} %copy-done, f32[16,2,64,128]{3,2,1,0:T(8,128)} %shard_map.140, f32[16,2,64,128]{3,2,1,0:T(8,128)S(1)} %copy-done.1, f32[16,2,64,128]{3,2,1,0:T(8,128)S(1)} %copy-done.2), kind=kLoop, calls=%fused_computation.2 | loop fusion | flops 3145728 | bytes 7340032 | tf_op jit(solution)/shard_map/sub | solution.py:692
Async XLA Ops:
  38.2 61.1 %copy-start = (f32[16,2,64,128]{3,2,1,0:T(8,128)S(1)}, f32[16,2,64,128]{3,2,1,0:T(8,128)}, u32[]{:S(2)}) copy-start(f32[16,2,64,128]{3,2,1,0:T(8,128)} %refs_3_.1) | copy-start | bytes 3145732
  38.2 61.0 %copy-start.1 = (f32[16,2,64,128]{3,2,1,0:T(8,128)S(1)}, f32[16,2,64,128]{3,2,1,0:T(8,128)}, u32[]{:S(2)}) copy-start(f32[16,2,64,128]{3,2,1,0:T(8,128)} %param.14) | copy-start | bytes 3145732
  38.2 61.0 %copy-start.2 = (f32[16,2,64,128]{3,2,1,0:T(8,128)S(1)}, f32[16,2,64,128]{3,2,1,0:T(8,128)}, u32[]{:S(2)}) copy-start(f32[16,2,64,128]{3,2,1,0:T(8,128)} %param.15) | copy-start | bytes 3145732

commit v5 on v4

--- a/solution.py
+++ b/solution.py
@@ -150,12 +150,13 @@
         for t in range(1, self.slab):
             self.near_copy(step, rows, part, near, sems, t).start()
 
-    def to_owner(self, steps, part, near, total, got, sems):
+    def to_owner(self, halves, steps, part, near, total, got, sems):
         far_send, far_recv = sems[2:]
         dp, slab, me_d, me_s = self.dp, self.slab, self.me_d, self.me_s
-        area, some = self.area // 2, self.per_k // 2
+        area, some = self.area // halves, self.per_k // halves
         rows = part.shape[1] // steps
-        chans = part.shape[1] // self.count // 2
+        chans = part.shape[1] // self.count // halves
+        parts = [n + c * halves for n in range(halves) for c in range(2)]
         owners = self.group // self.per_j
         first = lax.div(lax.rem(me_d + 1, dp), owners)
 
@@ -168,9 +169,9 @@
                 far_send.at[h, d], far_recv.at[h, me_d], d, me_s,
             )
 
-        for h in range(2):
-
-            @pl.loop(h * steps // 2, (h + 1) * steps // 2)
+        for h in range(halves):
+
+            @pl.loop(h * steps // halves, (h + 1) * steps // halves)
             def _(step):
                 for t in range(1, slab):
                     self.near_copy(step, rows, part, near, sems, t).wait_recv()
@@ -188,7 +189,7 @@
                     place = (g % self.per_j) * some
                     d = q * owners + g // self.per_j
                     total[h, d, place : place + some, :] = jnp.concatenate(
-                        [block[n * some : (n + 1) * some] for n in (0, 2, 1, 3)], axis=1
+                        [block[n * some : (n + 1) * some] for n in parts], axis=1
                     )
                 for g in range(owners):
                     d = q * owners + g
@@ -199,7 +200,7 @@
 
             got[place_of(h, me_d), :] = total[h, me_d]
 
-        for h in range(2):
+        for h in range(halves):
 
             @pl.loop(0, dp - 1)
             def _(n):
@@ -217,7 +218,7 @@
         @pl.loop(0, dp - 1)
         def _(n):
             d = lax.rem(me_d + 1 + n, dp)
-            for h in range(2):
+            for h in range(halves):
                 far_copy(h, d).wait_send()
 
     def owned(self, got, r):
@@ -343,7 +344,7 @@
             mixer[r] = jnp.concatenate([top, rest], axis=1)
 
         each(area, prepare)
-        links.to_owner(steps, part, near, total, got, sems[:4])
+        links.to_owner(2, steps, part, near, total, got, sems[:4])
         scale = 1.0 / math.sqrt(NY * NZ) / math.sqrt(KY * KZ)
 
         def mix(pair):
@@ -388,21 +389,18 @@
                 left[r] = jnp.concatenate([top, top, rest], axis=1)
 
         each(area // 2, prepare)
-        links.to_owner(steps, part, near, total, got, sems)
+        links.to_owner(1, steps, part, near, total, got, sems)
         scale = 1.0 / math.sqrt(NY * NZ) / math.sqrt(KY * KZ) / dp
 
-        def multiply(pair):
-            for r, g in links.owned(got, pair):
-                g = jnp.concatenate(
-                    [g[:, n * few : (n + 1) * few] for n in (0, 2, 1, 3)], axis=1
-                )
-                low = lax.broadcasted_iota(jnp.int32, g.shape, 1) < chans
-                turned = halves_swapped(g)
-                top, rest = split(jnp.concatenate([g, jnp.where(low, turned, -turned)], axis=0))
-                grad = mm(left[r], jnp.concatenate([top, rest, top], axis=0))
-                grad_ref[lax.rem(r, links.per_k), lax.div(r, links.per_k)] = grad * scale
-
-        each(area // 2, multiply)
+        def multiply(r):
+            g = got[pl.ds(r, dp, stride=area), :]
+            low = lax.broadcasted_iota(jnp.int32, g.shape, 1) < chans
+            turned = halves_swapped(g)
+            top, rest = split(jnp.concatenate([g, jnp.where(low, turned, -turned)], axis=0))
+            grad = mm(left[r], jnp.concatenate([top, rest, top], axis=0))
+            grad_ref[lax.rem(r, links.per_k), lax.div(r, links.per_k)] = grad * scale
+
+        each(area, multiply)
 
 
 def point_kernel(
@@ -535,14 +533,14 @@
     return pl.BlockSpec(shape, lambda i: (0,) * len(shape))
 
 
-def link_scratch(dp, slab, chans):
+def link_scratch(halves, dp, slab, chans):
     area = (KY // dp) * (KZ // slab)
     rows = chans * KY * (KZ // slab) // 64
     wide = 2 * chans
     return [
         pltpu.VMEM((slab, rows, 128), jnp.float32),
         pltpu.VMEM((slab - 1, rows, 128), jnp.float32),
-        pltpu.VMEM((2, dp, area // 2, wide), jnp.float32),
+        pltpu.VMEM((halves, dp, area // halves, wide), jnp.float32),
         pltpu.VMEM((dp * area, wide), jnp.float32),
     ]
 
@@ -580,7 +578,7 @@
             jax.ShapeDtypeStruct((chans * PAIRS, 4 * KZ), jnp.float32),
             jax.ShapeDtypeStruct((dp * area, wide), jnp.float32),
         ],
-        scratch_shapes=link_scratch(dp, slab, chans)
+        scratch_shapes=link_scratch(2, dp, slab, chans)
         + [
             pltpu.VMEM((area, wide, 2 * wide), jnp.bfloat16),
             pltpu.VMEM((dp * area, wide), jnp.float32),
@@ -613,9 +611,9 @@
         ],
         out_specs=whole((per_k, per_j, chans, 2 * chans)),
         out_shape=jax.ShapeDtypeStruct((per_k, per_j, chans, 2 * chans), jnp.float32),
-        scratch_shapes=link_scratch(dp, slab, chans)
+        scratch_shapes=link_scratch(1, dp, slab, chans)
         + [pltpu.VMEM((per_j * per_k, chans, 6 * dp), jnp.bfloat16)]
-        + link_sems(slab, chans // 2 // per, (2, dp)),
+        + link_sems(slab, chans // 2 // per, (1, dp)),
         compiler_params=pltpu.CompilerParams(
             vmem_limit_bytes=vmem_bytes, collective_id=1, has_side_effects=True
         ),

time: 103 us -> 102 us (level)
  Pallas kernels: 98.6 us -> 97.1 us
    pallas_call x1, Pallas kernels: 22.5 us -> 21 us  [grad_part(): pl.pallas_call(kernel, grid=(pairs // per,), in_specs=[pl.BlockSpec((per,...]
where the time goes in v5:
time: 102 us; the launch traced here: 101 us
  Pallas kernels  97.1 us (95%)
  other arithmetic  3.51 us (3%)
    pallas_call x1, Pallas kernels, point_part(): pl.pallas_call(point_kernel, grid=(rows // ROWS,), in_specs=[pl.BlockSpec...  38.5 us
    pallas_call x1, Pallas kernels, forward_part(): pl.pallas_call(kernel, grid=(chans // 2 // per,), in_specs=[pl.BlockSpec(...  37.6 us
    pallas_call x1, Pallas kernels, grad_part(): pl.pallas_call(kernel, grid=(pairs // per,), in_specs=[pl.BlockSpec((per,...  21 us
    sub x1, other arithmetic, body(): w_spec - 0.01 * (new_first / bias_first) / (jnp.sqrt(new_second / bias_se...  3.51 us

profile of v5, /device:TPU:1, one launch (start us, length us, event | category | flops | bytes accessed | tf_op | source)
XLA Modules:
  0.0 101.3 jit_solution(18445851171549949529)
XLA Ops:
  0.6 37.6 %shard_map.138 = (f32[1024,128]{1,0:T(8,128)}, f32[512,128]{1,0:T(8,128)}) custom-call(bf16[32,2,256,512]{3,2,1,0:T(8,128)(2,1)} %bitcast.4, bf16[2048,256]{1,0:T(8,128)(2,1)} %constant.27.clone.refs_1_.zt_ref, bf16[2,128,256]{2,1,0:T(8,128)(2,1)} %constant.28.clone.refs_2_.refs_1_, f32[16,2,64,128]{3,2,1,0:T(8,128)} %refs_3_.1), custom_call_target="tpu_custom_call" | custom-call | tf_op jit(solution)/shard_map/pallas_call | solution.py:567
  38.2 0.0 copy-start
  38.2 0.0 copy-start.1
  38.2 0.0 copy-start.2
  38.3 38.5 %shard_map.139 = (bf16[32,2,256,512]{3,2,1,0:T(8,128)(2,1)}, bf16[32,256,256]{2,1,0:T(8,128)(2,1)}) custom-call(bf16[64,256,512]{2,1,0:T(8,128)(2,1)} %bitcast.5, bf16[32,2,256,512]{3,2,1,0:T(8,128)(2,1)} %bitcast.6, f32[1024,128]{1,0:T(8,128)} %get-tuple-element.8.spec_ref, f32[64]{0:T(128)} %bias_ref.1, bf16[64,64]{1,0:T(8,128)(2,1)} %skip_ref.1, ...), custom_call_target="tpu_custom_call" | custom-call | tf_op jit(solution)/shard_map/pallas_call | solution.py:628
  76.8 21.0 %shard_map.140 = f32[16,2,64,128]{3,2,1,0:T(8,128)} custom-call(bf16[32,256,256]{2,1,0:T(8,128)(2,1)} %get-tuple-element.10.refs_0_, bf16[2,128,256]{2,1,0:T(8,128)(2,1)} %constant.28.clone.refs_2_.refs_1_, f32[512,128]{1,0:T(8,128)} %get-tuple-element.11.refs_2_), custom_call_target="tpu_custom_call" | custom-call | tf_op jit(solution)/shard_map/pallas_call | solution.py:604
  97.8 0.0 copy-done
  97.8 0.0 copy-done.1
  97.8 0.0 copy-done.2
  97.8 3.5 %divide_subtract_fusion = (f32[16,2,64,128]{3,2,1,0:T(8,128)}, f32[16,2,64,128]{3,2,1,0:T(8,128)}, f32[16,2,64,128]{3,2,1,0:T(8,128)}) fusion(f32[16,2,64,128]{3,2,1,0:T(8,128)S(1)} %copy-done, f32[16,2,64,128]{3,2,1,0:T(8,128)} %shard_map.140, f32[16,2,64,128]{3,2,1,0:T(8,128)S(1)} %copy-done.1, f32[16,2,64,128]{3,2,1,0:T(8,128)S(1)} %copy-done.2), kind=kLoop, calls=%fused_computation.2 | loop fusion | flops 3145728 | bytes 7340032 | tf_op jit(solution)/shard_map/sub | solution.py:690
Async XLA Ops:
  38.2 59.6 %copy-start = (f32[16,2,64,128]{3,2,1,0:T(8,128)S(1)}, f32[16,2,64,128]{3,2,1,0:T(8,128)}, u32[]{:S(2)}) copy-start(f32[16,2,64,128]{3,2,1,0:T(8,128)} %refs_3_.1) | copy-start | bytes 3145732
  38.2 59.6 %copy-start.1 = (f32[16,2,64,128]{3,2,1,0:T(8,128)S(1)}, f32[16,2,64,128]{3,2,1,0:T(8,128)}, u32[]{:S(2)}) copy-start(f32[16,2,64,128]{3,2,1,0:T(8,128)} %param.14) | copy-start | bytes 3145732
  38.2 59.6 %copy-start.2 = (f32[16,2,64,128]{3,2,1,0:T(8,128)S(1)}, f32[16,2,64,128]{3,2,1,0:T(8,128)}, u32[]{:S(2)}) copy-start(f32[16,2,64,128]{3,2,1,0:T(8,128)} %param.15) | copy-start | bytes 3145732

commit v6 on v5

--- a/solution.py
+++ b/solution.py
@@ -56,7 +56,7 @@
 
 
 def each(count, step):
-    per = math.gcd(count, 8)
+    per = math.gcd(count, 16)
 
     @pl.loop(0, count // per)
     def _(i):
@@ -150,7 +150,7 @@
         for t in range(1, self.slab):
             self.near_copy(step, rows, part, near, sems, t).start()
 
-    def to_owner(self, halves, steps, part, near, total, got, sems):
+    def to_owner(self, halves, steps, part, near, total, got, sems, meanwhile):
         far_send, far_recv = sems[2:]
         dp, slab, me_d, me_s = self.dp, self.slab, self.me_d, self.me_s
         area, some = self.area // halves, self.per_k // halves
@@ -199,6 +199,8 @@
                         far_copy(h, d).start()
 
             got[place_of(h, me_d), :] = total[h, me_d]
+            if h == halves - 2:
+                meanwhile()
 
         for h in range(halves):
 
@@ -343,8 +345,9 @@
             top, rest = split(both)
             mixer[r] = jnp.concatenate([top, rest], axis=1)
 
-        each(area, prepare)
-        links.to_owner(2, steps, part, near, total, got, sems[:4])
+        links.to_owner(
+            2, steps, part, near, total, got, sems[:4], lambda: each(area, prepare)
+        )
         scale = 1.0 / math.sqrt(NY * NZ) / math.sqrt(KY * KZ)
 
         def mix(pair):
@@ -389,7 +392,7 @@
                 left[r] = jnp.concatenate([top, top, rest], axis=1)
 
         each(area // 2, prepare)
-        links.to_owner(1, steps, part, near, total, got, sems)
+        links.to_owner(1, steps, part, near, total, got, sems, None)
         scale = 1.0 / math.sqrt(NY * NZ) / math.sqrt(KY * KZ) / dp
 
         def multiply(r):

time: 102 us -> 100 us (0.980)
  Pallas kernels: 97.1 us -> 95.8 us
    pallas_call x1, Pallas kernels: 38.5 us -> 37.3 us  [point_part(): pl.pallas_call(point_kernel, grid=(rows // ROWS,), in_specs=[pl.BlockSpec...]
where the time goes in v6:
time: 100 us
  Pallas kernels  95.8 us (96%)
  other arithmetic  3.51 us (4%)
    pallas_call x1, Pallas kernels, point_part(): pl.pallas_call(point_kernel, grid=(rows // ROWS,), in_specs=[pl.BlockSpec...  37.3 us
    pallas_call x1, Pallas kernels, forward_part(): pl.pallas_call(kernel, grid=(chans // 2 // per,), in_specs=[pl.BlockSpec(...  37 us
    pallas_call x1, Pallas kernels, grad_part(): pl.pallas_call(kernel, grid=(pairs // per,), in_specs=[pl.BlockSpec((per,...  21.5 us
    sub x1, other arithmetic, body(): w_spec - 0.01 * (new_first / bias_first) / (jnp.sqrt(new_second / bias_se...  3.51 us

profile of v6, /device:TPU:1, one launch (start us, length us, event | category | flops | bytes accessed | tf_op | source)
XLA Modules:
  0.0 100.0 jit_solution(17849393258993388589)
XLA Ops:
  0.6 37.0 %shard_map.138 = (f32[1024,128]{1,0:T(8,128)}, f32[512,128]{1,0:T(8,128)}) custom-call(bf16[32,2,256,512]{3,2,1,0:T(8,128)(2,1)} %bitcast.4, bf16[2048,256]{1,0:T(8,128)(2,1)} %constant.27.clone.refs_1_.zt_ref, bf16[2,128,256]{2,1,0:T(8,128)(2,1)} %constant.28.clone.refs_2_.refs_1_, f32[16,2,64,128]{3,2,1,0:T(8,128)} %refs_3_.1), custom_call_target="tpu_custom_call" | custom-call | tf_op jit(solution)/shard_map/pallas_call | solution.py:570
  37.7 0.0 copy-start
  37.7 0.0 copy-start.1
  37.7 0.0 copy-start.2
  37.7 37.3 %shard_map.139 = (bf16[32,2,256,512]{3,2,1,0:T(8,128)(2,1)}, bf16[32,256,256]{2,1,0:T(8,128)(2,1)}) custom-call(bf16[64,256,512]{2,1,0:T(8,128)(2,1)} %bitcast.5, bf16[32,2,256,512]{3,2,1,0:T(8,128)(2,1)} %bitcast.6, f32[1024,128]{1,0:T(8,128)} %get-tuple-element.8.spec_ref, f32[64]{0:T(128)} %bias_ref.1, bf16[64,64]{1,0:T(8,128)(2,1)} %skip_ref.1, ...), custom_call_target="tpu_custom_call" | custom-call | tf_op jit(solution)/shard_map/pallas_call | solution.py:631
  75.0 21.5 %shard_map.140 = f32[16,2,64,128]{3,2,1,0:T(8,128)} custom-call(bf16[32,256,256]{2,1,0:T(8,128)(2,1)} %get-tuple-element.10.refs_0_, bf16[2,128,256]{2,1,0:T(8,128)(2,1)} %constant.28.clone.refs_2_.refs_1_, f32[512,128]{1,0:T(8,128)} %get-tuple-element.11.refs_2_), custom_call_target="tpu_custom_call" | custom-call | tf_op jit(solution)/shard_map/pallas_call | solution.py:607
  96.5 0.0 copy-done
  96.5 0.0 copy-done.1
  96.5 0.0 copy-done.2
  96.5 3.5 %divide_subtract_fusion = (f32[16,2,64,128]{3,2,1,0:T(8,128)}, f32[16,2,64,128]{3,2,1,0:T(8,128)}, f32[16,2,64,128]{3,2,1,0:T(8,128)}) fusion(f32[16,2,64,128]{3,2,1,0:T(8,128)S(1)} %copy-done, f32[16,2,64,128]{3,2,1,0:T(8,128)} %shard_map.140, f32[16,2,64,128]{3,2,1,0:T(8,128)S(1)} %copy-done.1, f32[16,2,64,128]{3,2,1,0:T(8,128)S(1)} %copy-done.2), kind=kLoop, calls=%fused_computation.2 | loop fusion | flops 3145728 | bytes 7340032 | tf_op jit(solution)/shard_map/sub | solution.py:693
Async XLA Ops:
  37.7 58.8 %copy-start = (f32[16,2,64,128]{3,2,1,0:T(8,128)S(1)}, f32[16,2,64,128]{3,2,1,0:T(8,128)}, u32[]{:S(2)}) copy-start(f32[16,2,64,128]{3,2,1,0:T(8,128)} %refs_3_.1) | copy-start | bytes 3145732
  37.7 58.8 %copy-start.1 = (f32[16,2,64,128]{3,2,1,0:T(8,128)S(1)}, f32[16,2,64,128]{3,2,1,0:T(8,128)}, u32[]{:S(2)}) copy-start(f32[16,2,64,128]{3,2,1,0:T(8,128)} %param.14) | copy-start | bytes 3145732
  37.7 58.8 %copy-start.2 = (f32[16,2,64,128]{3,2,1,0:T(8,128)S(1)}, f32[16,2,64,128]{3,2,1,0:T(8,128)}, u32[]{:S(2)}) copy-start(f32[16,2,64,128]{3,2,1,0:T(8,128)} %param.15) | copy-start | bytes 3145732
